TPU v7x, 512 devices: a whole 4x8x8 slice. The times are simulated.
512 devices in a mesh: group: 8 (over z_hi, core), seq: 64 (over x, y, z_lo).
Axes of the slice: x: 4, y: 8, z: 8 (z_hi: 4, z_lo: 2; z = z_hi * 2 + z_lo), core: 2. Of those that a mesh axis runs over, the one named last changes fastest.
Arguments:
- latent_cache: bfloat16 [16, 16384, 576], P('group', 'seq'), may hold values from -6 to 6
- lengths: int32 [16], replicated, may hold values from 6553 to 16384, as said below
- moves: int32 [12, 4], replicated, may hold values from 0 to 7, as said below
- query_before: bfloat16 [16, 128, 576], P('group', 'seq'), may hold values from -256 to 256
- query_after: bfloat16 [32, 128, 576], P('group', 'seq'), may hold values from -256 to 256
Outputs:
- attended_before: bfloat16 [16, 128, 512], P('group', 'seq')
- lse_before: float32 [16, 128], P('group', 'seq')
- attended_after: bfloat16 [32, 128, 512], P('group', 'seq')
- lse_after: float32 [32, 128], P('group', 'seq')
- moved_cache: bfloat16 [16, 16384, 576], P('group', 'seq')
Inputs may be any that keep to these rules, and one draw needn't show every extreme that they name: `lengths`: some request has exactly 16384 tokens and some exactly the least. Source group differs from destination group; no two moves share a source slot, a destination group and receiving slot, or a pair of source and destination groups; every group sends and receives at most 2 requests, and some group receives 2.
All inputs are finite; a program needn't handle non-finite values.
Results may differ from a plain program's by a relative error of at most 0.0054.
Values may be sent and summed in bfloat16 or wider, within the bound.
A program may use at most 64 MiB of HBM per device.

v0:
```python
import jax
import jax.numpy as jnp
from jax import lax
from jax.sharding import PartitionSpec as P

LAT = 512


SCALE = 192.0 ** (-0.5)


def broadcast(value, axis, source):
    kept = jnp.where(lax.axis_index(axis) == source, value, 0).astype(value.dtype)
    return lax.psum(kept, axis)


def decode(queries, cache, length, positions, seat):
    scores = (
        jnp.einsum(
            "rhc,rtc->rht",
            lax.all_gather(queries, "seq", axis=1, tiled=True),
            cache,
            preferred_element_type=jnp.float32,
        )
        * SCALE
    )
    live = (positions[None, :] < length[:, None])[:, None, :]
    masked = jnp.where(live, scores, jnp.float32(-1e30))
    top = lax.pmax(jnp.max(masked, axis=2), "seq")
    weights = jnp.where(live, jnp.exp(masked - top[:, :, None]), jnp.float32(0.0))
    total = jnp.sum(weights, axis=2)
    numer = jnp.einsum(
        "rht,rtc->rhc",
        weights.astype(jnp.bfloat16),
        cache[:, :, :LAT],
        preferred_element_type=jnp.float32,
    )
    numer, total = (
        lax.psum_scatter(numer, "seq", scatter_dimension=1, tiled=True),
        lax.psum_scatter(total, "seq", scatter_dimension=1, tiled=True),
    )
    heads_mine = queries.shape[1]
    top_mine = lax.dynamic_slice_in_dim(top, seat * heads_mine, heads_mine, 1)
    empty = (length == 0).astype(jnp.float32)[:, None]
    attended = (numer / (total + empty)[:, :, None]).astype(jnp.bfloat16)
    lse = jnp.where(length[:, None] > 0, top_mine + jnp.log(total + empty), jnp.float32(0.0))
    return (attended, lse)


def local(latent_cache, lengths, moves, query_before, query_after):
    group = lax.axis_index("group")
    seat = lax.axis_index("seq")
    req = latent_cache.shape[0]
    shard = latent_cache.shape[1]
    width = latent_cache.shape[2]
    spare = query_after.shape[0] - req
    positions = seat * shard + jnp.arange(shard, dtype=jnp.int32)
    mine = lax.dynamic_slice_in_dim(lengths, group * req, req)
    src_group = moves[:, 0]
    src_slot = moves[:, 1]
    dst_group = moves[:, 2]
    dst_spare = moves[:, 3]
    slots = jnp.arange(req, dtype=jnp.int32)
    leaving = jnp.any((src_group == group)[None, :] & (src_slot[None, :] == slots[:, None]), axis=1)
    resident_len = jnp.where(leaving, 0, mine)
    every_row = jnp.arange(lengths.shape[0], dtype=jnp.int32)
    anchor = src_group * req + src_slot
    anchor_len = jnp.sum(
        jnp.where(every_row[None, :] == anchor[:, None], lengths[None, :], 0), axis=1
    )
    receive = jnp.arange(spare, dtype=jnp.int32)
    landing = (dst_group == group)[None, :] & (dst_spare[None, :] == receive[:, None])
    arrival_len = jnp.sum(jnp.where(landing, anchor_len[None, :], 0), axis=1)
    length_after = jnp.concatenate([resident_len, arrival_len])
    before_out, before_lse = decode(query_before, latent_cache, mine, positions, seat)

    def carry_one(step, store):
        piece = lax.dynamic_index_in_dim(latent_cache, src_slot[step], 0, keepdims=False)
        got = broadcast(piece, "group", src_group[step])
        current = lax.dynamic_index_in_dim(store, dst_spare[step], 0, keepdims=False)
        chosen = jnp.where(dst_group[step] == group, got, current)
        return lax.dynamic_update_index_in_dim(store, chosen, dst_spare[step], 0)

    start = jnp.zeros((spare, shard, width), jnp.bfloat16)
    arrived = lax.fori_loop(0, moves.shape[0], carry_one, start)
    combined = jnp.concatenate([latent_cache, arrived], axis=0)
    after_out, after_lse = decode(query_after, combined, length_after, positions, seat)
    return (before_out, before_lse, after_out, after_lse, arrived)


def solution(mesh):
    placed = (P("group", "seq", None), P(), P(), P("group", "seq", None), P("group", "seq", None))
    return jax.shard_map(
        local,
        mesh=mesh,
        in_specs=placed,
        out_specs=(
            P("group", "seq", None),
            P("group", "seq"),
            P("group", "seq", None),
            P("group", "seq"),
            P("group", "seq", None),
        ),
        check_vma=False,
    )
```

profile of v0, /device:TPU:8, one launch (start us, length us, event | category | flops | bytes accessed | tf_op | source)
XLA Modules:
  0.0 2105.9 jit_solution(5312739817988085136)
XLA Ops:
  8.0 1.4 copy.36
  9.5 0.8 constant_dynamic-update-slice_fusion.2
  11.1 166.5 %all_gather.7 = bf16[4,128,576]{2,0,1:T(4,128)(2,1)} all-gather(bf16[4,2,576]{2,0,1:T(4,128)(2,1)S(1)} %copy.39), channel_id=1, replica_groups=mesh['group'=8,'seq'=64] {'seq'}, dimensions={1}, use_global_device_ids=true | all-gather | bytes 599040 | tf_op jit(solution)/shard_map/all_gather | solution.py:21
  177.6 161.5 %all_gather.6 = bf16[2,128,576]{2,0,1:T(2,128)(2,1)} all-gather(bf16[2,2,576]{2,0,1:T(2,128)(2,1)S(1)} %copy.34), channel_id=1, replica_groups=mesh['group'=8,'seq'=64] {'seq'}, dimensions={1}, use_global_device_ids=true | all-gather | bytes 299520 | tf_op jit(solution)/shard_map/all_gather | solution.py:21
  339.2 988.0 %while.15 = (s32[]{:T(128)}, bf16[2,256,576]{1,2,0:T(8,128)(2,1)S(1)}, s32[12]{0:T(128)S(1)}, s32[]{:T(128)}, s32[12]{0:T(128)S(1)}, /*index=5*/s32[12]{0:T(128)...) while((s32[]{:T(128)}, ...), condition=%wide.region_10.11_spmd, body=%wide.region_8.10_spmd.sunk | while | flops 442381 | bytes 5669209 | solution.py:85
  343.1 0.8 select_bitcast_fusion.2
  347.9 76.1 %all-reduce.12.cloned.1.call-done = bf16[256,576]{1,0:T(8,128)(2,1)} async-done(((bf16[256,576]{1,0:T(8,128)(2,1)}), bf16[256,576]{1,0:T(8,128)(2,1)}) %all-reduce.12.cloned.1.call-update) | async-done | bytes 294928 | tf_op jit(solution)/shard_map/while/body/eval_jaxpr/psum | solution.py:14
  432.8 73.1 %all-reduce.12.cloned.1.call-done = bf16[256,576]{1,0:T(8,128)(2,1)} async-done(((bf16[256,576]{1,0:T(8,128)(2,1)}), bf16[256,576]{1,0:T(8,128)(2,1)}) %all-reduce.12.cloned.1.call-update) | async-done | bytes 294928 | tf_op jit(solution)/shard_map/while/body/eval_jaxpr/psum | solution.py:14
  510.0 0.8 select_bitcast_fusion.2
  514.8 73.0 %all-reduce.12.cloned.1.call-done = bf16[256,576]{1,0:T(8,128)(2,1)} async-done(((bf16[256,576]{1,0:T(8,128)(2,1)}), bf16[256,576]{1,0:T(8,128)(2,1)}) %all-reduce.12.cloned.1.call-update) | async-done | bytes 294928 | tf_op jit(solution)/shard_map/while/body/eval_jaxpr/psum | solution.py:14
  591.9 0.8 select_bitcast_fusion.2
  596.7 73.1 %all-reduce.12.cloned.1.call-done = bf16[256,576]{1,0:T(8,128)(2,1)} async-done(((bf16[256,576]{1,0:T(8,128)(2,1)}), bf16[256,576]{1,0:T(8,128)(2,1)}) %all-reduce.12.cloned.1.call-update) | async-done | bytes 294928 | tf_op jit(solution)/shard_map/while/body/eval_jaxpr/psum | solution.py:14
  678.7 73.8 %all-reduce.12.cloned.1.call-done = bf16[256,576]{1,0:T(8,128)(2,1)} async-done(((bf16[256,576]{1,0:T(8,128)(2,1)}), bf16[256,576]{1,0:T(8,128)(2,1)}) %all-reduce.12.cloned.1.call-update) | async-done | bytes 294928 | tf_op jit(solution)/shard_map/while/body/eval_jaxpr/psum | solution.py:14
  761.4 74.0 %all-reduce.12.cloned.1.call-done = bf16[256,576]{1,0:T(8,128)(2,1)} async-done(((bf16[256,576]{1,0:T(8,128)(2,1)}), bf16[256,576]{1,0:T(8,128)(2,1)}) %all-reduce.12.cloned.1.call-update) | async-done | bytes 294928 | tf_op jit(solution)/shard_map/while/body/eval_jaxpr/psum | solution.py:14
  835.4 1.0 fusion.34
  845.3 72.1 %all-reduce.12.cloned.1.call-done = bf16[256,576]{1,0:T(8,128)(2,1)} async-done(((bf16[256,576]{1,0:T(8,128)(2,1)}), bf16[256,576]{1,0:T(8,128)(2,1)}) %all-reduce.12.cloned.1.call-update) | async-done | bytes 294928 | tf_op jit(solution)/shard_map/while/body/eval_jaxpr/psum | solution.py:14
  926.2 73.1 %all-reduce.12.cloned.1.call-done = bf16[256,576]{1,0:T(8,128)(2,1)} async-done(((bf16[256,576]{1,0:T(8,128)(2,1)}), bf16[256,576]{1,0:T(8,128)(2,1)}) %all-reduce.12.cloned.1.call-update) | async-done | bytes 294928 | tf_op jit(solution)/shard_map/while/body/eval_jaxpr/psum | solution.py:14
  1008.1 73.0 %all-reduce.12.cloned.1.call-done = bf16[256,576]{1,0:T(8,128)(2,1)} async-done(((bf16[256,576]{1,0:T(8,128)(2,1)}), bf16[256,576]{1,0:T(8,128)(2,1)}) %all-reduce.12.cloned.1.call-update) | async-done | bytes 294928 | tf_op jit(solution)/shard_map/while/body/eval_jaxpr/psum | solution.py:14
  1090.1 73.0 %all-reduce.12.cloned.1.call-done = bf16[256,576]{1,0:T(8,128)(2,1)} async-done(((bf16[256,576]{1,0:T(8,128)(2,1)}), bf16[256,576]{1,0:T(8,128)(2,1)}) %all-reduce.12.cloned.1.call-update) | async-done | bytes 294928 | tf_op jit(solution)/shard_map/while/body/eval_jaxpr/psum | solution.py:14
  1172.0 73.0 %all-reduce.12.cloned.1.call-done = bf16[256,576]{1,0:T(8,128)(2,1)} async-done(((bf16[256,576]{1,0:T(8,128)(2,1)}), bf16[256,576]{1,0:T(8,128)(2,1)}) %all-reduce.12.cloned.1.call-update) | async-done | bytes 294928 | tf_op jit(solution)/shard_map/while/body/eval_jaxpr/psum | solution.py:14
  1253.9 73.1 %all-reduce.12.cloned.1.call-done = bf16[256,576]{1,0:T(8,128)(2,1)} async-done(((bf16[256,576]{1,0:T(8,128)(2,1)}), bf16[256,576]{1,0:T(8,128)(2,1)}) %all-reduce.12.cloned.1.call-update) | async-done | bytes 294928 | tf_op jit(solution)/shard_map/while/body/eval_jaxpr/psum | solution.py:14
  1327.3 0.8 constant_dynamic-update-slice_fusion.1
  1328.9 0.9 copy-done.2
  1330.5 153.2 %all-reduce.6 = (f32[2,128]{1,0:T(2,128)S(1)}, f32[4,128]{1,0:T(4,128)S(1)}) all-reduce(f32[2,128]{1,0:T(2,128)S(1)} %get-tuple-element.280, f32[4,128]{1,0:T(4,128)S(1)} %get-tuple-element.282), channel_id=1, replica_groups=mesh['group'=8,'seq'=64] {'seq'}, use_global_device_ids=true, to_apply=%region_1.2 | all-reduce | flops 768 | bytes 6144 | tf_op jit(solution)/shard_map/pmax | solution.py:29
  1483.7 0.9 fusion.4
  1484.6 1.7 copy.43
  1486.3 1.1 fusion.7
  1487.8 1.3 dynamic-slice
  1489.9 302.9 %all-reduce.4 = (f32[2,128]{1,0:T(2,128)S(1)}, f32[4,128]{0,1:T(8,128)S(1)}) all-reduce(f32[2,128]{1,0:T(2,128)S(1)} %fusion.16, f32[4,128]{0,1:T(8,128)S(1)} %copy.44), channel_id=3, replica_groups=mesh['group'=8,'seq'=64] {'seq'}, use_global_device_ids=true, to_apply=%region_4.5.clone | all-reduce | flops 768 | bytes 6144
  1794.4 301.3 %all-reduce.10.cloned.1.call-done = (f32[2,128,512]{2,1,0:T(8,128)}, f32[4,128,512]{2,0,1:T(4,128)}) async-done(((f32[2,128,512]{2,1,0:T(8,128)}, f32[4,128,512]{2,0,1:T(4,128)}), (f32[2,128,512]{2,1,0:T(8,128)}, f32[4,128,512]{2,0,1:T(4,128)})) %all-reduce.10.cloned.1.call-update) | async-done | bytes 1572880
  2095.7 0.8 fusion.22
  2097.1 1.4 fusion.23
  (187 shorter events, 46.2 us)
Async XLA Ops:
  8.0 1.5 copy-start.1
  8.0 2.3 copy-start.7
  8.0 2.3 copy-start.8
  8.0 3.1 copy-start.5
  9.5 168.2 %copy-start.6 = (bf16[2,2,576]{2,1,0:T(2,128)(2,1)S(1)}, bf16[2,2,576]{2,1,0:T(2,128)(2,1)}, u32[]{:S(2)}) copy-start(bf16[2,2,576]{2,1,0:T(2,128)(2,1)} %param.10) | copy-start | bytes 13828
  339.2 84.7 %all-reduce.12.cloned.1.call-start = ((), (), s32[]{:S(2)}) async-start(), calls=%async_computation.1 | async-start | bytes 655360 | tf_op jit(solution)/shard_map/while/body/eval_jaxpr/psum | solution.py:14
  424.2 81.7 %all-reduce.12.cloned.1.call-start = ((), (), s32[]{:S(2)}) async-start(), calls=%async_computation.1 | async-start | bytes 655360 | tf_op jit(solution)/shard_map/while/body/eval_jaxpr/psum | solution.py:14
  506.2 81.7 %all-reduce.12.cloned.1.call-start = ((), (), s32[]{:S(2)}) async-start(), calls=%async_computation.1 | async-start | bytes 655360 | tf_op jit(solution)/shard_map/while/body/eval_jaxpr/psum | solution.py:14
  588.1 81.7 %all-reduce.12.cloned.1.call-start = ((), (), s32[]{:S(2)}) async-start(), calls=%async_computation.1 | async-start | bytes 655360 | tf_op jit(solution)/shard_map/while/body/eval_jaxpr/psum | solution.py:14
  670.1 82.4 %all-reduce.12.cloned.1.call-start = ((), (), s32[]{:S(2)}) async-start(), calls=%async_computation.1 | async-start | bytes 655360 | tf_op jit(solution)/shard_map/while/body/eval_jaxpr/psum | solution.py:14
  752.7 82.7 %all-reduce.12.cloned.1.call-start = ((), (), s32[]{:S(2)}) async-start(), calls=%async_computation.1 | async-start | bytes 655360 | tf_op jit(solution)/shard_map/while/body/eval_jaxpr/psum | solution.py:14
  836.6 80.7 %all-reduce.12.cloned.1.call-start = ((), (), s32[]{:S(2)}) async-start(), calls=%async_computation.1 | async-start | bytes 655360 | tf_op jit(solution)/shard_map/while/body/eval_jaxpr/psum | solution.py:14
  917.6 81.7 %all-reduce.12.cloned.1.call-start = ((), (), s32[]{:S(2)}) async-start(), calls=%async_computation.1 | async-start | bytes 655360 | tf_op jit(solution)/shard_map/while/body/eval_jaxpr/psum | solution.py:14
  999.5 81.7 %all-reduce.12.cloned.1.call-start = ((), (), s32[]{:S(2)}) async-start(), calls=%async_computation.1 | async-start | bytes 655360 | tf_op jit(solution)/shard_map/while/body/eval_jaxpr/psum | solution.py:14
  1081.4 81.7 %all-reduce.12.cloned.1.call-start = ((), (), s32[]{:S(2)}) async-start(), calls=%async_computation.1 | async-start | bytes 655360 | tf_op jit(solution)/shard_map/while/body/eval_jaxpr/psum | solution.py:14
  1163.3 81.7 %all-reduce.12.cloned.1.call-start = ((), (), s32[]{:S(2)}) async-start(), calls=%async_computation.1 | async-start | bytes 655360 | tf_op jit(solution)/shard_map/while/body/eval_jaxpr/psum | solution.py:14
  1245.3 81.7 %all-reduce.12.cloned.1.call-start = ((), (), s32[]{:S(2)}) async-start(), calls=%async_computation.1 | async-start | bytes 655360 | tf_op jit(solution)/shard_map/while/body/eval_jaxpr/psum | solution.py:14
  1327.2 1.6 copy-start
  1327.2 768.4 %all-reduce.10.cloned.1.call-start = ((), (), s32[]{:S(2)}) async-start(), calls=%async_computation | async-start | bytes 3145728
  1327.3 1.2 copy-start.4
  1327.3 1.6 copy-start.3
  1328.5 1.3 copy-start.2
Sparse Core Ops, SparseCore 0:
  344.0 79.9 all-reduce.11
  428.9 76.9 all-reduce.11
  510.9 76.8 all-reduce.11
  592.8 76.9 all-reduce.11
  674.8 77.6 all-reduce.11
  757.5 77.8 all-reduce.11
  841.4 75.9 all-reduce.11
  922.3 76.9 all-reduce.11
  1004.2 76.8 all-reduce.11
  1086.2 76.8 all-reduce.11
  1168.1 76.8 all-reduce.11
  1250.0 76.9 all-reduce.11
Sparse Core Ops, SparseCore 1:
  1487.5 608.1 all-reduce.9
where the time goes:
time: 2110 us
  waiting for transfers between devices  1180 us (56%)
  blocking collectives  784 us (37%)
  loops' own time  63.1 us (3%)
  local copies, waits for them, and re-layouts  42.3 us (2%)
    psum x12, waiting for transfers between devices, broadcast(): return lax.psum(kept, axis)  880 us
    all_gather x2, blocking collectives, decode(): lax.all_gather(queries, 'seq', axis=1, tiled=True)  328 us
    unnamed x1, blocking collectives  303 us
    unnamed x2, waiting for transfers between devices  301 us
    pmax x1, blocking collectives, decode(): top = lax.pmax(jnp.max(masked, axis=2), 'seq')  153 us
    another operation x1, loops' own time, local(): arrived = lax.fori_loop(0, moves.shape[0], carry_one, start)  63.1 us
  transfers between devices with their start and end apart: 13, of which 13 were waited for; matrix products, arithmetic and copies ran while one was open for 1% of the time, Pallas kernels for 0%

commit v1 on v0

v1 whole, which is shorter than its diff:
```python
import jax
import jax.numpy as jnp
from jax import lax
from jax.experimental import pallas as pl
from jax.experimental.pallas import tpu as pltpu
from jax.sharding import PartitionSpec as P

MESH = pl.DeviceIdType.MESH
LAT = 512
SCALE = 192.0 ** (-0.5)
LOW = -1e30
NX, NY, NZ, NG = 4, 8, 8, 8
F32, BF16 = jnp.float32, jnp.bfloat16


def loop(lo, hi, body):
    def step(i, carry):
        body(i)
        return carry

    lax.fori_loop(lo, hi, step, 0)


def to_column(row, n, offset):
    lane = lax.broadcasted_iota(jnp.int32, (n, 128), 1)
    sub = lax.broadcasted_iota(jnp.int32, (n, 128), 0)
    picked = jnp.where(lane == sub + offset, jnp.broadcast_to(row, (n, 128)), 0.0)
    return jnp.sum(picked, axis=1, keepdims=True)


def merge(parts, stats, n, offset):
    top = stats[0]
    for s in stats[1:]:
        top = jnp.maximum(top, s)
    weights = [jnp.exp(s - top) for s in stats]
    total = weights[0]
    for w in weights[1:]:
        total = total + w
    scale = 1.0 / total
    out = None
    for part, w in zip(parts, weights):
        term = to_column(w * scale, n, offset) * part.astype(F32)
        out = term if out is None else out + term
    return out, top + jnp.log(total)


def kernel(lens, moves, cache, qb, qa, ob, lb, oa, la, moved,
           cv, st, sel, rq, pb, pa, bs, g0, g1,
           s10, r10, t10, u10, s11, r11, t11, u11,
           s20, r20, t20, u20, s21, r21, t21, u21,
           s3, r3, b3, t3, u3,
           lsem, p1s, p1r, p2s, p2r, zs, zr, as_, ar, xs, xr, ms, mr, ns, nr, os_, or_):
    req, shard, width = cv.shape
    piece = shard // NG
    g, s = lax.axis_index("group"), lax.axis_index("seq")
    zh, core = g // 2, g % 2
    x, y, zl = s // (2 * NY), (s // 2) % NY, s % 2
    v = (zh * 2 + zl) * 2 + core

    def ring(w):
        z, c = w // 2, w % 2
        return {"group": (z // 2) * 2 + c, "seq": (x * NY + y) * 2 + z % 2}

    def at_group(h):
        return {"group": h, "seq": s}

    def at_x(i):
        return {"group": g, "seq": (i * NY + y) * 2 + zl}

    def at_y(i):
        return {"group": g, "seq": (x * NY + i) * 2 + zl}

    vp = ((zh * 2 + (1 - zl)) * 2) + core

    def remote(src, dst, ss, rs, dev):
        return pltpu.make_async_remote_copy(
            src_ref=src, dst_ref=dst, send_sem=ss, recv_sem=rs, device_id=dev, device_id_type=MESH
        )

    load = pltpu.make_async_copy(cache, cv, lsem.at[0])
    load.start()
    barrier = pltpu.get_barrier_semaphore()

    def greet(dev):
        pl.semaphore_signal(barrier, inc=1, device_id=dev, device_id_type=MESH)

    loop(1, 16, lambda d: greet(ring((v + d) % 16)))
    loop(1, NY, lambda d: greet(at_y((y + d) % NY)))
    loop(1, NX, lambda d: greet(at_x((x + d) % NX)))

    zero = jnp.zeros((1, 128), F32)
    for i in range(NX):
        t10[i], u10[i], t21[i], u21[i] = zero, zero, zero, zero
    for i in range(NY):
        t11[i], u11[i], t20[i], u20[i] = zero, zero, zero, zero
    for r in range(req):
        t3[r] = zero
    rq[v] = qa[req:]
    table = [[moves[i, c] for c in range(4)] for i in range(moves.shape[0])]

    def look(match):
        a = b = c = jnp.int32(0)
        for m in table:
            hit = match(m)
            a = a + jnp.where(hit, m[0] * req + m[1], 0)
            b = b + jnp.where(hit, m[2] * req + m[3], 0)
            c = c + jnp.where(hit, 1, 0)
        return a, b, c > 0

    out_to = [look(lambda m, r=r: (m[0] == g) & (m[1] == r)) for r in range(req)]
    came = [look(lambda m, k=k: (m[2] == g) & (m[3] == k)) for k in range(req)]
    load.wait()
    pl.semaphore_wait(barrier, 15 + NY - 1 + NX - 1)

    def z1(d):
        return remote(qa.at[pl.ds(req, req)], rq.at[v], zs.at[d], zr.at[d], ring((v + d) % 16))

    zq = remote(qb, pb, zs.at[0], zr.at[0], ring(vp))
    zp = remote(qa.at[pl.ds(0, req)], pa, zs.at[16], zr.at[16], ring(vp))
    zq.start()
    zp.start()
    loop(1, 16, lambda d: z1(d).start())

    def p1(d):
        h = (g + d) % NG
        return remote(cv.at[:, pl.ds(h * piece, piece), :], st.at[g], p1s.at[d], p1r.at[d], at_group(h))

    loop(1, NG, lambda d: p1(d).start())
    keep = pltpu.make_async_copy(cv.at[:, pl.ds(g * piece, piece), :], st.at[g], lsem.at[1])
    keep.start()

    zq.wait()
    zp.wait()
    loop(1, 16, lambda d: z1(d).wait())
    for r in range(req):
        _, target, leaves = out_to[r]
        for i in range(2):
            mine = zl == i
            before = jnp.where(mine, qb[r].astype(F32), pb[r].astype(F32))
            stay = jnp.where(mine, qa[r].astype(F32), pa[r].astype(F32))
            tg = target // req
            away = rq[((tg // 2) * 2 + i) * 2 + tg % 2, target % req].astype(F32)
            bs[r, 4 * i : 4 * i + 2] = before
            bs[r, 4 * i + 2 : 4 * i + 4] = jnp.where(leaves, away, stay)
    g0[x, y] = bs[0].astype(BF16)
    g1[y, x] = bs[1].astype(BF16)

    def a0(d):
        return remote(g0.at[x, y], g0.at[x, y], as_.at[d], ar.at[d], at_y((y + d) % NY))

    def a1(d):
        return remote(g1.at[y, x], g1.at[y, x], as_.at[NY + d], ar.at[NY + d], at_x((x + d) % NX))

    def b0(d):
        return remote(g0.at[x], g0.at[x], xs.at[d], xr.at[d], at_x((x + d) % NX))

    def b1(d):
        return remote(g1.at[y], g1.at[y], xs.at[NX + d], xr.at[NX + d], at_y((y + d) % NY))

    loop(1, NX, lambda d: a1(d).start())
    loop(1, NY, lambda d: a0(d).start())
    loop(1, NX, lambda d: a1(d).wait())
    loop(1, NY, lambda d: b1(d).start())
    loop(1, NY, lambda d: a0(d).wait())
    loop(1, NX, lambda d: b0(d).start())

    position = s * shard + lax.broadcasted_iota(jnp.int32, (shard, 1), 0)
    length = [lens[g * req + r] for r in range(req)]

    def attend(q, r):
        n = q.shape[0]
        scores = lax.dot_general(
            cv[r], q, (((1,), (1,)), ((), ())), preferred_element_type=F32
        ) * SCALE
        live = jnp.broadcast_to(position, (shard, n)) < length[r]
        masked = jnp.where(live, scores, LOW)
        top = jnp.max(masked, axis=0, keepdims=True)
        weights = jnp.where(live, jnp.exp(masked - top), 0.0)
        total = jnp.sum(weights, axis=0, keepdims=True)
        some = total > 0.0
        safe = jnp.where(some, total, 1.0)
        part = lax.dot_general(
            (weights * (1.0 / safe)).astype(BF16), cv[r, :, :LAT],
            (((0,), (0,)), ((), ())), preferred_element_type=F32,
        )
        return part.astype(BF16), jnp.where(some, top + jnp.log(safe), LOW)

    def rows(block):
        a, b, w = block.shape
        return block.astype(F32).reshape(a * b, w).astype(BF16)

    n0, n1 = NY * 8, NX * 8

    def c0(d):
        to = (x + d) % NX
        return (remote(s10.at[to], r10.at[x], ms.at[0, d], mr.at[0, d], at_x(to)),
                remote(t10.at[to], u10.at[x], ms.at[1, d], mr.at[1, d], at_x(to)))

    def c1(d):
        to = (y + d) % NY
        return (remote(s11.at[to], r11.at[y], ms.at[2, d], mr.at[2, d], at_y(to)),
                remote(t11.at[to], u11.at[y], ms.at[3, d], mr.at[3, d], at_y(to)))

    def each(copies, what):
        for c in copies:
            getattr(c, what)()

    part, lse = attend(rows(g1[y]), 1)
    r11[y] = part
    u11[y, :, 0:n1] = lse
    part, lse = attend(rows(g0[x]), 0)
    r10[x] = part
    u10[x, :, 0:n0] = lse

    keep.wait()
    loop(1, NG, lambda d: p1(d).wait())

    def pick(i):
        d, k = i // req, i % req
        a, _, found = look(lambda m: (m[2] == d) & (m[3] == k))
        value = st[a // req, a % req]
        sel[d, k] = jnp.where(found, value, jnp.zeros_like(value))

    loop(0, NG * req, pick)

    def p2(d):
        h = (g + d) % NG
        return remote(sel.at[h], moved.at[:, pl.ds(g * piece, piece), :], p2s.at[d], p2r.at[d], at_group(h))

    loop(1, NG, lambda d: p2(d).start())
    own = pltpu.make_async_copy(sel.at[g], moved.at[:, pl.ds(g * piece, piece), :], lsem.at[2])
    own.start()

    def block1(d):
        b1(d).wait_recv()
        frm = (y + NY - d) % NY
        part, lse = attend(rows(g1[frm]), 1)
        s11[frm] = part
        t11[frm, :, 0:n1] = lse
        each(c1(NY - d), "start")

    def block0(d):
        b0(d).wait_recv()
        frm = (x + NX - d) % NX
        part, lse = attend(rows(g0[frm]), 0)
        s10[frm] = part
        t10[frm, :, 0:n0] = lse
        each(c0(NX - d), "start")

    loop(1, NX, block0)
    loop(1, NY, block1)

    loop(1, NX, lambda d: b0(d).wait_send())
    loop(1, NY, lambda d: b1(d).wait_send())

    def e0(d):
        to = (y + d) % NY
        return (remote(s20.at[to], r20.at[y], ns.at[0, d], nr.at[0, d], at_y(to)),
                remote(t20.at[0], u20.at[y], ns.at[1, d], nr.at[1, d], at_y(to)))

    def e1(d):
        to = (x + d) % NX
        return (remote(s21.at[to], r21.at[x], ns.at[2, d], nr.at[2, d], at_x(to)),
                remote(t21.at[0], u21.at[x], ns.at[3, d], nr.at[3, d], at_x(to)))

    loop(1, NX, lambda d: each(c0(d), "wait"))
    part, lse = merge([r10[i] for i in range(NX)], [u10[i] for i in range(NX)], n0, 0)
    s20[...] = part.reshape(NY, 8, LAT).astype(BF16)
    t20[0] = lse
    r20[y] = s20[y]
    u20[y] = lse
    loop(1, NY, lambda d: each(e0(d), "start"))

    loop(1, NY, lambda d: each(c1(d), "wait"))
    part, lse = merge([r11[i] for i in range(NY)], [u11[i] for i in range(NY)], n1, 0)
    s21[...] = part.reshape(NX, 8, LAT).astype(BF16)
    t21[0] = lse
    r21[x] = s21[x]
    u21[x] = lse
    loop(1, NX, lambda d: each(e1(d), "start"))

    loop(1, NX, lambda d: each(e1(d), "wait"))
    part1, lse1 = merge([r21[i] for i in range(NX)], [u21[i] for i in range(NX)], 8, 8 * x)
    loop(1, NY, lambda d: each(e0(d), "wait"))
    part0, lse0 = merge([r20[i] for i in range(NY)], [u20[i] for i in range(NY)], 8, 8 * y)
    t3[0] = pltpu.roll(jnp.broadcast_to(lse0, (8, 128)), (128 - 8 * y) % 128, 1)[0:1]
    t3[1] = pltpu.roll(jnp.broadcast_to(lse1, (8, 128)), (128 - 8 * x) % 128, 1)[0:1]
    for r, part in enumerate((part0, part1)):
        for i in range(2):
            for b in range(2):
                s3[i, b, r] = part[4 * i + 2 * b : 4 * i + 2 * b + 2]

    def f(d):
        w = (v + d) % 16
        return (remote(s3.at[(w // 2) % 2, 1], r3.at[v], os_.at[0, d], or_.at[0, d], ring(w)),
                remote(t3, u3.at[v], os_.at[1, d], or_.at[1, d], ring(w)))

    fb = remote(s3.at[1 - zl, 0], b3, os_.at[0, 0], or_.at[0, 0], ring(vp))
    fb.start()
    loop(1, 16, lambda d: each(f(d), "start"))
    r3[v] = s3[zl, 1]
    u3[v] = t3[...]
    fb.wait()
    loop(1, 16, lambda d: each(f(d), "wait"))

    def turned(row):
        return pltpu.roll(jnp.broadcast_to(row, (8, 128)), (128 - 4 * zl) % 128, 1)[0:1]

    def shifted(row):
        return pltpu.roll(jnp.broadcast_to(row, (8, 128)), 126, 1)[0:1]

    for r in range(req):
        stats = [turned(u3[v, r]), turned(u3[vp, r])]
        alive = length[r] > 0
        out, lse = merge([s3[zl, 0, r], b3[r]], stats, 2, 0)
        ob[r] = jnp.where(alive, out, 0.0).astype(BF16)
        lb[r : r + 1, :] = jnp.where(alive, lse, 0.0)[:, 0:2]
        stays = alive & jnp.logical_not(out_to[r][2])
        out, lse = merge([r3[v, r], r3[vp, r]], stats, 2, 2)
        oa[r] = jnp.where(stays, out, 0.0).astype(BF16)
        la[r : r + 1, :] = shifted(jnp.where(stays, lse, 0.0))[:, 0:2]
    for k in range(req):
        a, _, found = came[k]
        sg, sl = a // req, a % req
        w = [((sg // 2) * 2 + i) * 2 + sg % 2 for i in range(2)]
        stats = [turned(u3[j, sl]) for j in w]
        alive = found & (lens[a] > 0)
        out, lse = merge([r3[j, sl] for j in w], stats, 2, 2)
        oa[req + k] = jnp.where(alive, out, 0.0).astype(BF16)
        la[req + k : req + k + 1, :] = shifted(jnp.where(alive, lse, 0.0))[:, 0:2]

    own.wait()
    loop(1, NG, lambda d: p2(d).wait())


def local(cache, lengths, moves, qb, qa):
    req, shard, width = cache.shape
    heads = qb.shape[1]
    piece = shard // NG
    n0, n1 = NY * 8, NX * 8
    vm, dma = pltpu.VMEM, pltpu.SemaphoreType.DMA
    spec = pl.BlockSpec(memory_space=pltpu.VMEM)
    smem = pl.BlockSpec(memory_space=pltpu.SMEM)
    anywhere = pl.BlockSpec(memory_space=pl.ANY)
    shape = jax.ShapeDtypeStruct
    return pl.pallas_call(
        kernel,
        out_shape=(
            shape((req, heads, LAT), BF16),
            shape((req, heads), F32),
            shape((2 * req, heads, LAT), BF16),
            shape((2 * req, heads), F32),
            shape((req, shard, width), BF16),
        ),
        in_specs=[smem, smem, anywhere, spec, spec],
        out_specs=(spec, spec, spec, spec, anywhere),
        scratch_shapes=[
            vm((req, shard, width), BF16),
            vm((NG, req, piece, width), BF16),
            vm((NG, req, piece, width), BF16),
            vm((16, req, heads, width), BF16),
            vm((req, heads, width), BF16),
            vm((req, heads, width), BF16),
            vm((req, 8, width), F32),
            vm((NX, NY, 8, width), BF16),
            vm((NY, NX, 8, width), BF16),
            vm((NX, n0, LAT), BF16), vm((NX, n0, LAT), BF16), vm((NX, 1, 128), F32), vm((NX, 1, 128), F32),
            vm((NY, n1, LAT), BF16), vm((NY, n1, LAT), BF16), vm((NY, 1, 128), F32), vm((NY, 1, 128), F32),
            vm((NY, 8, LAT), BF16), vm((NY, 8, LAT), BF16), vm((NY, 1, 128), F32), vm((NY, 1, 128), F32),
            vm((NX, 8, LAT), BF16), vm((NX, 8, LAT), BF16), vm((NX, 1, 128), F32), vm((NX, 1, 128), F32),
            vm((2, 2, req, heads, LAT), F32),
            vm((16, req, heads, LAT), F32),
            vm((req, heads, LAT), F32),
            vm((req, 1, 128), F32),
            vm((16, req, 1, 128), F32),
            dma((3,)),
            dma((NG,)), dma((NG,)), dma((NG,)), dma((NG,)),
            dma((17,)), dma((17,)),
            dma((NY + NX,)), dma((NY + NX,)),
            dma((NX + NY,)), dma((NX + NY,)),
            dma((4, NY)), dma((4, NY)),
            dma((4, NY)), dma((4, NY)),
            dma((2, 16)), dma((2, 16)),
        ],
        name="decode_and_move",
        compiler_params=pltpu.CompilerParams(
            collective_id=0, has_side_effects=True, vmem_limit_bytes=32 << 20
        ),
    )(lengths, moves, cache, qb, qa)


def solution(mesh):
    placed = (P("group", "seq", None), P(), P(), P("group", "seq", None), P("group", "seq", None))
    return jax.shard_map(
        local,
        mesh=mesh,
        in_specs=placed,
        out_specs=(
            P("group", "seq", None),
            P("group", "seq"),
            P("group", "seq", None),
            P("group", "seq"),
            P("group", "seq", None),
        ),
        check_vma=False,
    )
```

time: 2110 us -> 67.2 us (0.03)
  the two profiles are of different devices: /device:TPU:8 before, /device:TPU:1 now
where the time goes in v1:
time: 67.2 us; the launch traced here: 67 us
  Pallas kernels  60.7 us (90%)
  local copies, waits for them, and re-layouts  5.64 us (8%)
    pallas_call x1, Pallas kernels, local(): pl.pallas_call(kernel, out_shape=(shape((req, heads, LAT), BF16), shape((...  60.7 us
    unnamed x11, local copies, waits for them, and re-layouts  3.93 us
    pallas_call x2, local copies, waits for them, and re-layouts, local(): pl.pallas_call(kernel, out_shape=(shape((req, heads, LAT), BF16), shape((...  1.71 us

profile of v1, /device:TPU:1, one launch (start us, length us, event | category | flops | bytes accessed | tf_op | source)
XLA Modules:
  0.0 67.0 jit_solution(17151572747166428265)
XLA Ops:
  0.6 0.8 %copy.10.moves = s32[12,4]{1,0:T(8,128)S(1)} copy(s32[12,4]{0,1:T(4,128)} %param.7) | data formatting | bytes 384 | tf_op args[2]
  1.4 0.0 copy-start
  1.4 0.0 copy-start.1
  1.4 0.0 copy-start.2
  1.4 1.4 %copy.11.cache = bf16[2,256,576]{2,1,0:T(8,128)(2,1)S(1)} copy(bf16[2,256,576]{1,2,0:T(8,128)(2,1)} %param.5) | data formatting | bytes 1179648 | tf_op args[0]
  2.8 0.0 copy-done
  2.8 0.0 copy-done.1
  2.8 0.0 copy-done.2
  2.8 60.7 %decode_and_move.1 = (bf16[2,2,512]{2,1,0:T(2,128)(2,1)S(1)}, f32[2,2]{1,0:T(2,128)S(1)}, bf16[4,2,512]{2,1,0:T(2,128)(2,1)S(1)}, f32[4,2]{1,0:T(4,128)S(1)}, bf16[2,256,576]{2,1,0:T(8,128)(2,1)S(1)}) custom-call(s32[16]{0:T(128)S(1)} %copy-done.2, s32[12,4]{1,0:T(8,128)S(1)} %copy.10.moves, bf16[2,256,576]{2,1,0:T(8,128)(2,1)S(1)} %copy.11.cache, ...), custom_call_target="tpu_custom_call" | custom-call | tf_op jit(solution)/shard_map/decode_and_move/pallas_call | solution.py:346
  63.5 0.6 copy.12
  64.2 1.1 %copy.13 = bf16[2,256,576]{1,2,0:T(8,128)(2,1)} copy(bf16[2,256,576]{2,1,0:T(8,128)(2,1)S(1)} %get-tuple-element.9) | data formatting | bytes 1179648 | tf_op jit(solution)/shard_map/decode_and_move/pallas_call | solution.py:346
  65.2 0.6 copy.17
  65.8 0.6 copy.18
  66.4 0.6 copy.19
Async XLA Ops:
  1.4 1.4 %copy-start = (bf16[4,2,576]{2,1,0:T(2,128)(2,1)S(1)}, bf16[4,2,576]{2,1,0:T(2,128)(2,1)}, u32[]{:S(2)}) copy-start(bf16[4,2,576]{2,1,0:T(2,128)(2,1)} %qa.1) | copy-start | bytes 27652
  1.4 1.4 %copy-start.1 = (bf16[2,2,576]{2,1,0:T(2,128)(2,1)S(1)}, bf16[2,2,576]{2,1,0:T(2,128)(2,1)}, u32[]{:S(2)}) copy-start(bf16[2,2,576]{2,1,0:T(2,128)(2,1)} %qb.1) | copy-start | bytes 13828
  1.4 1.4 %copy-start.2 = (s32[16]{0:T(128)S(1)}, s32[16]{0:T(128)}, u32[]{:S(2)}) copy-start(s32[16]{0:T(128)} %lens.1) | copy-start | bytes 196

commit v2 on v0

v2 whole, which is shorter than its diff:
```python
import jax
import jax.numpy as jnp
from jax import lax
from jax.experimental import pallas as pl
from jax.experimental.pallas import tpu as pltpu
from jax.sharding import PartitionSpec as P

MESH = pl.DeviceIdType.MESH
LAT = 512
SCALE = 192.0 ** (-0.5)
LOW = -1e30
NX, NY, NZ, NG = 4, 8, 8, 8
F32, BF16 = jnp.float32, jnp.bfloat16


def loop(lo, hi, body):
    for i in range(lo, hi):
        body(i)


def div(a, b):
    return lax.div(a, jnp.int32(b))


def rem(a, b):
    return lax.rem(a, jnp.int32(b))


def to_column(row, n):
    lane = lax.broadcasted_iota(jnp.int32, (n, 128), 1)
    sub = lax.broadcasted_iota(jnp.int32, (n, 128), 0)
    picked = jnp.where(lane == sub, jnp.broadcast_to(row, (n, 128)), 0.0)
    return jnp.sum(picked, axis=1, keepdims=True)


def to_row(column):
    n = column.shape[0]
    lane = lax.broadcasted_iota(jnp.int32, (n, 128), 1)
    sub = lax.broadcasted_iota(jnp.int32, (n, 128), 0)
    spread = jnp.where(lane == sub, jnp.broadcast_to(column, (n, 128)), 0.0)
    return jnp.sum(spread, axis=0, keepdims=True)


def weigh(stats):
    top = stats[0]
    for s in stats[1:]:
        top = jnp.maximum(top, s)
    weights = [jnp.exp(s - top) for s in stats]
    total = weights[0]
    for w in weights[1:]:
        total = total + w
    scale = 1.0 / total
    return [w * scale for w in weights], top + jnp.log(total)


def blend(parts, columns):
    out = None
    for part, w in zip(parts, columns):
        term = w * part.astype(F32)
        out = term if out is None else out + term
    return out


def tail(column):
    n = column.shape[0]
    high = column.astype(BF16).astype(F32)
    rest = column - high
    mid = rest.astype(BF16).astype(F32)
    lane = lax.broadcasted_iota(jnp.int32, (n, 128), 1)
    terms = jnp.where(lane == 0, high, jnp.where(lane == 1, mid, jnp.where(lane == 2, rest - mid, 0.0)))
    return terms.astype(BF16)


def untail(block):
    return jnp.sum(block.astype(F32), axis=1, keepdims=True)


def join(blocks):
    weights, lse = weigh([untail(b[:, LAT:]) for b in blocks])
    return blend([b[:, :LAT] for b in blocks], weights), lse


def kernel(lens_h, moves_h, cache, qb_h, qa_h, ob, lb, oa, la, moved,
           lens, moves, qb, qa, cv, st0, st1, sel0, sel1, rq, pb, pa, bs, gq,
           s1, r1, t1, u1, s2, r2, s3, r3, b3,
           lsem, p1s, p1r, p2s, p2r, zs, zr, as_, ar, xs, xr, ms, mr, ns, nr, os_, or_):
    req, width, shard = cv.shape
    high = width // (NG // 2)
    st, sel = (st0, st1), (sel0, sel1)
    cuts = ((0, st0.shape[2]), (st0.shape[2], st1.shape[2]))
    g, s = lax.axis_index("group"), lax.axis_index("seq")
    zh, core = div(g, 2), rem(g, 2)
    x, y, zl = div(s, 2 * NY), rem(div(s, 2), NY), rem(s, 2)
    v = (zh * 2 + zl) * 2 + core

    def ring(w):
        z, c = div(w, 2), rem(w, 2)
        return {"group": div(z, 2) * 2 + c, "seq": (x * NY + y) * 2 + rem(z, 2)}

    def at_group(h):
        return {"group": h, "seq": s}

    def at_x(i):
        return {"group": g, "seq": (i * NY + y) * 2 + zl}

    def at_y(i):
        return {"group": g, "seq": (x * NY + i) * 2 + zl}

    vp = ((zh * 2 + (1 - zl)) * 2) + core
    far_x, far_y, far_z = (2, 1, 3), (4, 3, 5, 2, 6, 1, 7), (8, 9, 7, 6, 10, 5, 11, 4, 12, 3, 13, 2, 14, 1, 15)
    near_x = (1, 3, 2)

    def piece(ref, h, c):
        low, size = cuts[c]
        at = pl.multiple_of(div(h, 2) * high + low, 16)
        return ref.at[:, pl.ds(at, size), pl.ds(pl.multiple_of(rem(h, 2) * 128, 128), 128)]

    def remote(src, dst, ss, rs, dev):
        return pltpu.make_async_remote_copy(
            src_ref=src, dst_ref=dst, send_sem=ss, recv_sem=rs, device_id=dev, device_id_type=MESH
        )

    barrier = pltpu.get_barrier_semaphore()

    def greet(dev):
        pl.semaphore_signal(barrier, inc=1, device_id=dev, device_id_type=MESH)

    for d in far_z:
        greet(ring(rem(v + d, 16)))
    for d in far_y:
        greet(at_y(rem(y + d, NY)))
    for d in far_x:
        greet(at_x(rem(x + d, NX)))
    loads = [
        pltpu.make_async_copy(a, b, lsem.at[i])
        for i, (a, b) in enumerate(((qb_h, qb), (qa_h, qa), (cache, cv), (moves_h, moves), (lens_h, lens)))
    ]
    for copy in loads:
        copy.start()
    for copy in loads:
        copy.wait()
    pl.semaphore_wait(barrier, 15 + NY - 1 + NX - 1)

    def z1(d):
        return remote(qa.at[pl.ds(req, req)], rq.at[v], zs.at[d], zr.at[d], ring(rem(v + d, 16)))

    zq = remote(qb, pb, zs.at[0], zr.at[0], ring(vp))
    zp = remote(qa.at[pl.ds(0, req)], pa, zs.at[16], zr.at[16], ring(vp))
    zq.start()
    for d in far_z:
        z1(d).start()
    zp.start()

    def p1(d, c):
        h = rem(g + d, NG)
        return remote(piece(cv, h, c), st[c].at[g], p1s.at[c, d], p1r.at[c, d], at_group(h))

    for c in range(2):
        loop(1, NG, lambda d: p1(d, c).start())
    keep = [pltpu.make_async_copy(piece(cv, g, c), st[c].at[g], lsem.at[5 + c]) for c in range(2)]
    for copy in keep:
        copy.start()

    rq[v] = qa[req:]
    table = [[moves[c, i] for c in range(4)] for i in range(moves.shape[1])]

    def look(match):
        a = b = c = jnp.int32(0)
        for m in table:
            hit = match(m)
            a = a + jnp.where(hit, m[0] * req + m[1], 0)
            b = b + jnp.where(hit, m[2] * req + m[3], 0)
            c = c + jnp.where(hit, 1, 0)
        return a, b, c > 0

    out_to = [look(lambda m, r=r: (m[0] == g) & (m[1] == r)) for r in range(req)]
    came = [look(lambda m, k=k: (m[2] == g) & (m[3] == k)) for k in range(req)]
    length = [lens[g * req + r] for r in range(req)]

    def ga(u, d):
        return remote(gq.at[u, x, y], gq.at[u, x, y], as_.at[u, d], ar.at[u, d], at_y(rem(y + d, NY)))

    def gb(u, d):
        return remote(gq.at[u, x], gq.at[u, x], xs.at[u, d], xr.at[u, d], at_x(rem(x + d, NX)))

    zq.wait()
    for r in range(req):
        for i in range(2):
            mine = zl == i
            bs[0, 4 * i + 2 * r : 4 * i + 2 * r + 2] = jnp.where(mine, qb[r].astype(F32), pb[r].astype(F32))
    gq[0, x, y] = bs[0].astype(BF16)
    for d in far_y:
        ga(0, d).start()

    zp.wait()
    for d in far_z:
        z1(d).wait()
    for r in range(req):
        _, target, leaves = out_to[r]
        tg = div(target, req)
        for i in range(2):
            stay = jnp.where(zl == i, qa[r].astype(F32), pa[r].astype(F32))
            away = rq[(div(tg, 2) * 2 + i) * 2 + rem(tg, 2), rem(target, req)].astype(F32)
            bs[1, 4 * i + 2 * r : 4 * i + 2 * r + 2] = jnp.where(leaves, away, stay)
    gq[1, x, y] = bs[1].astype(BF16)
    for d in far_y:
        ga(1, d).start()

    n = NY * 8
    row = lax.broadcasted_iota(jnp.int32, (n, 1), 0)
    second = rem(div(row, 2), 2) == 1
    position = s * shard + lax.broadcasted_iota(jnp.int32, (n, shard), 1)

    def attend(u, i):
        q = gq[u, i].astype(F32).reshape(n, width).astype(BF16)
        scores = jnp.where(
            second,
            jnp.dot(q, cv[1], preferred_element_type=F32),
            jnp.dot(q, cv[0], preferred_element_type=F32),
        ) * SCALE
        live = position < jnp.where(second, length[1], length[0])
        masked = jnp.where(live, scores, LOW)
        top = jnp.max(masked, axis=1, keepdims=True)
        weights = jnp.where(live, jnp.exp(masked - top), 0.0)
        total = jnp.sum(weights, axis=1, keepdims=True)
        some = total > 0.0
        safe = jnp.where(some, total, 1.0)
        weights = weights * (1.0 / safe)
        part = None
        for r in range(req):
            mine = jnp.where(second == (r == 1), weights, 0.0).astype(BF16)
            term = lax.dot_general(
                mine, cv[r, :LAT, :], (((1,), (1,)), ((), ())), preferred_element_type=F32
            )
            part = term if part is None else part + term
        return part.astype(BF16), to_row(jnp.where(some, top + jnp.log(safe), LOW))

    def rc(u, d):
        to = rem(x + d, NX)
        return (remote(s1.at[u, to], r1.at[u, x], ms.at[u, 0, d], mr.at[u, 0, d], at_x(to)),
                remote(t1.at[u, to], u1.at[u, x], ms.at[u, 1, d], mr.at[u, 1, d], at_x(to)))

    def each(copies, what):
        for c in copies:
            getattr(c, what)()

    def own_block(u):
        r1[u, x], u1[u, x] = attend(u, x)

    def other_block(u, d):
        gb(u, d).wait_recv()
        frm = rem(x + NX - d, NX)
        s1[u, frm], t1[u, frm] = attend(u, frm)
        each(rc(u, NX - d), "start")

    def forward(c):
        keep[c].wait()
        loop(1, NG, lambda d: p1(d, c).wait())

        def pick(i, carry):
            d, k = div(i, req), rem(i, req)
            a, _, found = look(lambda m: (m[2] == d) & (m[3] == k))
            value = st[c][div(a, req), rem(a, req)]
            sel[c][d, k] = jnp.where(found, value, jnp.zeros_like(value))
            return carry

        lax.fori_loop(0, NG * req, pick, 0)
        loop(1, NG, lambda d: p2(d, c).start())
        own[c].start()

    def p2(d, c):
        h = rem(g + d, NG)
        return remote(sel[c].at[h], piece(moved, g, c), p2s.at[c, d], p2r.at[c, d], at_group(h))

    own = [pltpu.make_async_copy(sel[c].at[g], piece(moved, g, c), lsem.at[7 + c]) for c in range(2)]

    for d in far_y:
        ga(0, d).wait()
    for d in far_x:
        gb(0, d).start()
    own_block(0)
    for d in far_y:
        ga(1, d).wait()
    for d in far_x:
        gb(1, d).start()
    own_block(1)
    forward(0)
    for d in near_x:
        other_block(0, d)
    forward(1)
    for d in near_x:
        other_block(1, d)

    def re(u, d):
        to = rem(y + d, NY)
        return remote(s2.at[u, to], r2.at[u, y], ns.at[u, d], nr.at[u, d], at_y(to))

    def second_step(u):
        for d in near_x:
            gb(u, d).wait_send()
            each(rc(u, d), "wait")
        weights, lse = weigh([u1[u, i] for i in range(NX)])
        part = blend([r1[u, i] for i in range(NX)], [to_column(w, n) for w in weights])
        s2[u, :, :, :LAT] = part.reshape(NY, 8, LAT).astype(BF16)
        s2[u, :, :, LAT:] = tail(to_column(lse, n)).astype(F32).reshape(NY, 8, 128).astype(BF16)
        r2[u, y] = s2[u, y]
        for d in far_y:
            re(u, d).start()

    def third_step(u):
        for d in far_y:
            re(u, d).wait()
        part, lse = join([r2[u, i] for i in range(NY)])
        end = tail(lse)
        for i in range(2):
            for r in range(req):
                rows = slice(4 * i + 2 * r, 4 * i + 2 * r + 2)
                s3[u, i, r, :, :LAT] = part[rows].astype(BF16)
                s3[u, i, r, :, LAT:] = end[rows]

    second_step(0)
    second_step(1)

    def rf(d):
        w = rem(v + d, 16)
        return remote(s3.at[1, rem(div(w, 2), 2)], r3.at[v], os_.at[d], or_.at[d], ring(w))

    fb = remote(s3.at[0, 1 - zl], b3, os_.at[0], or_.at[0], ring(vp))
    third_step(0)
    fb.start()
    third_step(1)
    for d in far_z:
        rf(d).start()
    r3[v] = s3[1, zl]
    fb.wait()
    for r in range(req):
        out, lse = join([s3[0, zl, r], b3[r]])
        alive = length[r] > 0
        ob[r] = jnp.where(alive, out, 0.0).astype(BF16)
        lb[r : r + 1, :] = to_row(jnp.where(alive, lse, 0.0))[:, 0:2]
    for d in far_z:
        rf(d).wait()
    for r in range(req):
        out, lse = join([r3[v, r], r3[vp, r]])
        stays = (length[r] > 0) & jnp.logical_not(out_to[r][2])
        oa[r] = jnp.where(stays, out, 0.0).astype(BF16)
        la[:, r : r + 1] = jnp.where(stays, lse, 0.0)
    for k in range(req):
        a, _, found = came[k]
        sg, sl = div(a, req), rem(a, req)
        out, lse = join([r3[(div(sg, 2) * 2 + i) * 2 + rem(sg, 2), sl] for i in range(2)])
        alive = found & (lens[a] > 0)
        oa[req + k] = jnp.where(alive, out, 0.0).astype(BF16)
        la[:, req + k : req + k + 1] = jnp.where(alive, lse, 0.0)

    for c in range(2):
        own[c].wait()
        loop(1, NG, lambda d: p2(d, c).wait())


def place(*refs):
    n = len(refs) // 3
    sems = refs[-1]
    parts = []
    for i, (a, c, b) in enumerate(zip(refs[:n], refs[n : 2 * n], refs[2 * n : 3 * n])):
        parts.append((pltpu.make_async_copy(a, b, sems.at[0, i]), pltpu.make_async_copy(b, c, sems.at[1, i])))
    for a, _ in parts:
        a.start()
    for a, b in parts:
        a.wait()
        b.start()
    for _, b in parts:
        b.wait()


def local(cache, lengths, moves, qb, qa):
    req, shard, width = cache.shape
    heads = qb.shape[1]
    high = width // (NG // 2)
    first = high // 32 * 16 + 16
    n = NY * 8
    wide = LAT + 128
    vm, dma = pltpu.VMEM, pltpu.SemaphoreType.DMA
    spec = pl.BlockSpec(memory_space=pltpu.VMEM)
    hbm = pl.BlockSpec(memory_space=pltpu.HBM)
    anywhere = pl.BlockSpec(memory_space=pl.ANY)
    shape = jax.ShapeDtypeStruct
    outs = (
        shape((req, heads, LAT), BF16),
        shape((req, heads), F32),
        shape((2 * req, heads, LAT), BF16),
        shape((heads, 2 * req), F32),
        shape((req, width, shard), BF16),
    )
    got = pl.pallas_call(
        kernel,
        out_shape=outs,
        in_specs=[hbm] * 5,
        out_specs=(spec, spec, spec, spec, anywhere),
        scratch_shapes=[
            pltpu.SMEM(lengths.shape, jnp.int32),
            pltpu.SMEM(moves.shape[::-1], jnp.int32),
            vm(qb.shape, BF16),
            vm(qa.shape, BF16),
            vm((req, width, shard), BF16),
            vm((NG, req, first, 128), BF16), vm((NG, req, high - first, 128), BF16),
            vm((NG, req, first, 128), BF16), vm((NG, req, high - first, 128), BF16),
            vm((16, req, heads, width), BF16),
            vm((req, heads, width), BF16),
            vm((req, heads, width), BF16),
            vm((2, 8, width), F32),
            vm((2, NX, NY, 8, width), BF16),
            vm((2, NX, n, LAT), BF16), vm((2, NX, n, LAT), BF16),
            vm((2, NX, 1, 128), F32), vm((2, NX, 1, 128), F32),
            vm((2, NY, 8, wide), BF16), vm((2, NY, 8, wide), BF16),
            vm((2, 2, req, heads, wide), BF16),
            vm((16, req, heads, wide), BF16),
            vm((req, heads, wide), BF16),
            dma((9,)),
            dma((2, NG)), dma((2, NG)), dma((2, NG)), dma((2, NG)),
            dma((17,)), dma((17,)),
            dma((2, NY)), dma((2, NY)),
            dma((2, NX)), dma((2, NX)),
            dma((2, 2, NX)), dma((2, 2, NX)),
            dma((2, NY)), dma((2, NY)),
            dma((16,)), dma((16,)),
        ],
        name="decode_and_move",
        compiler_params=pltpu.CompilerParams(
            collective_id=0, has_side_effects=True, vmem_limit_bytes=63 << 20
        ),
    )(lengths, moves.T, jnp.transpose(cache, (0, 2, 1)), qb, qa)
    ob, lb, oa, la, moved = pl.pallas_call(
        place,
        out_shape=outs,
        in_specs=[hbm] * 5,
        out_specs=(hbm,) * 5,
        scratch_shapes=[*(vm(o.shape, o.dtype) for o in outs), dma((2, 5))],
        name="place",
        compiler_params=pltpu.CompilerParams(vmem_limit_bytes=63 << 20),
    )(*got)
    return ob, lb, oa, la.T, jnp.transpose(moved, (0, 2, 1))


def solution(mesh):
    placed = (P("group", "seq", None), P(), P(), P("group", "seq", None), P("group", "seq", None))
    return jax.shard_map(
        local,
        mesh=mesh,
        in_specs=placed,
        out_specs=(
            P("group", "seq", None),
            P("group", "seq"),
            P("group", "seq", None),
            P("group", "seq"),
            P("group", "seq", None),
        ),
        check_vma=False,
    )
```

time: 2110 us -> 56.4 us (0.03)
  the two profiles are of different devices: /device:TPU:8 before, /device:TPU:1 now
where the time goes in v2:
time: 56.4 us; the launch traced here: 56.2 us
  Pallas kernels  55.6 us (99%)
  between operations  0.64 us (1%)
    pallas_call x1, Pallas kernels, local(): pl.pallas_call(kernel, out_shape=outs, in_specs=[hbm] * 5, out_specs=(spe...  53.6 us
    pallas_call x1, Pallas kernels, local(): pl.pallas_call(place, out_shape=outs, in_specs=[hbm] * 5, out_specs=(hbm,...  2 us

profile of v2, /device:TPU:1, one launch (start us, length us, event | category | flops | bytes accessed | tf_op | source)
XLA Modules:
  0.0 56.2 jit_solution(15346186351542672531)
XLA Ops:
  0.6 53.6 %decode_and_move.1 = (bf16[2,2,512]{2,1,0:T(2,128)(2,1)}, f32[2,2]{1,0:T(2,128)}, bf16[4,2,512]{2,1,0:T(2,128)(2,1)}, f32[2,4]{1,0:T(2,128)}, bf16[2,576,256]{2,1,0:T(8,128)(2,1)}) custom-call(s32[16]{0:T(128)} %lens_h.1, s32[4,12]{1,0:T(4,128)} %bitcast.5, bf16[2,576,256]{2,1,0:T(8,128)(2,1)} %bitcast.4, bf16[2,2,576]{2,1,0:T(2,128)(2,1)} %qb_h.1, ...), custom_call_target="tpu_custom_call" | custom-call | tf_op jit(solution)/shard_map/decode_and_move/pallas_call | solution.py:395
  54.2 2.0 %place.1 = (bf16[2,2,512]{2,1,0:T(2,128)(2,1)}, f32[2,2]{1,0:T(2,128)}, bf16[4,2,512]{2,1,0:T(2,128)(2,1)}, f32[2,4]{1,0:T(2,128)}, bf16[2,576,256]{2,1,0:T(8,128)(2,1)}) custom-call(bf16[2,2,512]{2,1,0:T(2,128)(2,1)} %get-tuple-element.15.refs_0_, f32[2,2]{1,0:T(2,128)} %get-tuple-element.16.refs_1_, bf16[4,2,512]{2,1,0:T(2,128)(2,1)} %get-tuple-element.17.refs_2_, ...), custom_call_target="tpu_custom_call" | custom-call | tf_op jit(solution)/shard_map/place/pallas_call | solution.py:433

commit v3 on v2

v3 whole, which is shorter than its diff:
```python
import jax
import jax.numpy as jnp
from jax import lax
from jax.experimental import pallas as pl
from jax.experimental.pallas import tpu as pltpu
from jax.sharding import PartitionSpec as P

MESH = pl.DeviceIdType.MESH
LAT = 512
SCALE = 192.0 ** (-0.5)
LOW = -1e30
CUTS = (48, 48, 48)
NX, NY, NZ, NG = 4, 8, 8, 8
F32, BF16 = jnp.float32, jnp.bfloat16


def loop(lo, hi, body):
    for i in range(lo, hi):
        body(i)


def div(a, b):
    return lax.div(a, jnp.int32(b))


def rem(a, b):
    return lax.rem(a, jnp.int32(b))


def to_column(row, n):
    lane = lax.broadcasted_iota(jnp.int32, (n, 128), 1)
    sub = lax.broadcasted_iota(jnp.int32, (n, 128), 0)
    picked = jnp.where(lane == sub, jnp.broadcast_to(row, (n, 128)), 0.0)
    return jnp.sum(picked, axis=1, keepdims=True)


def to_row(column):
    n = column.shape[0]
    lane = lax.broadcasted_iota(jnp.int32, (n, 128), 1)
    sub = lax.broadcasted_iota(jnp.int32, (n, 128), 0)
    spread = jnp.where(lane == sub, jnp.broadcast_to(column, (n, 128)), 0.0)
    return jnp.sum(spread, axis=0, keepdims=True)


def weigh(stats):
    top = stats[0]
    for s in stats[1:]:
        top = jnp.maximum(top, s)
    weights = [jnp.exp(s - top) for s in stats]
    total = weights[0]
    for w in weights[1:]:
        total = total + w
    scale = 1.0 / total
    return [w * scale for w in weights], top + jnp.log(total)


def blend(parts, columns):
    out = None
    for part, w in zip(parts, columns):
        term = w * part.astype(F32)
        out = term if out is None else out + term
    return out


def tail(column):
    n = column.shape[0]
    high = column.astype(BF16).astype(F32)
    rest = column - high
    mid = rest.astype(BF16).astype(F32)
    lane = lax.broadcasted_iota(jnp.int32, (n, 128), 1)
    terms = jnp.where(lane == 0, high, jnp.where(lane == 1, mid, jnp.where(lane == 2, rest - mid, 0.0)))
    return terms.astype(BF16)


def untail(block):
    return jnp.sum(block.astype(F32), axis=1, keepdims=True)


def join(blocks):
    weights, lse = weigh([untail(b[:, LAT:]) for b in blocks])
    return blend([b[:, :LAT] for b in blocks], weights), lse


def look(table, match):
    a = b = c = jnp.int32(0)
    for m in table:
        hit = match(m)
        a = a + jnp.where(hit, m[0] * 2 + m[1], 0)
        b = b + jnp.where(hit, m[2] * 2 + m[3], 0)
        c = c + jnp.where(hit, 1, 0)
    return a, b, c > 0


def read_table(moves):
    return [[moves[c, i] for c in range(4)] for i in range(moves.shape[1])]


def kernel(lens_h, moves_h, cache, qb_h, qa_h, kept, b3, r3, moved,
           lens, moves, qb, qa, cv, st, sel, rq, qx, pb, pa, bs, gq,
           s1, r1, t1, u1, s2, r2, s3, s4,
           lsem, p1s, p1r, p2s, p2r, zs, zr, as_, ar, xs, xr, ms, mr, ns, nr, os_, or_):
    req, width, shard = cv.shape
    high = width // (NG // 2)
    cuts, low = [], 0
    for ref in st:
        cuts.append((low, ref.shape[2]))
        low += ref.shape[2]
    n_cuts = len(cuts)
    g, s = lax.axis_index("group"), lax.axis_index("seq")
    zh, core = div(g, 2), rem(g, 2)
    x, y, zl = div(s, 2 * NY), rem(div(s, 2), NY), rem(s, 2)
    v = (zh * 2 + zl) * 2 + core

    def ring(w):
        z, c = div(w, 2), rem(w, 2)
        return {"group": div(z, 2) * 2 + c, "seq": (x * NY + y) * 2 + rem(z, 2)}

    def at_group(h):
        return {"group": h, "seq": s}

    def at_x(i):
        return {"group": g, "seq": (i * NY + y) * 2 + zl}

    def at_y(i):
        return {"group": g, "seq": (x * NY + i) * 2 + zl}

    vp = ((zh * 2 + (1 - zl)) * 2) + core
    far_x, far_y, far_z = (2, 1, 3), (4, 3, 5, 2, 6, 1, 7), (8, 9, 7, 6, 10, 5, 11, 4, 12, 3, 13, 2, 14, 1, 15)
    near_x = (1, 3, 2)

    def piece(ref, h, c):
        low, size = cuts[c]
        at = pl.multiple_of(div(h, 2) * high + low, 16)
        return ref.at[:, pl.ds(at, size), pl.ds(pl.multiple_of(rem(h, 2) * 128, 128), 128)]

    def remote(src, dst, ss, rs, dev):
        return pltpu.make_async_remote_copy(
            src_ref=src, dst_ref=dst, send_sem=ss, recv_sem=rs, device_id=dev, device_id_type=MESH
        )

    def arrived(ref, sem):
        remote(ref, ref, sem, sem, ring(vp)).wait_recv()

    def left(ref, sem):
        remote(ref, ref, sem, sem, ring(vp)).wait_send()

    barrier = pltpu.get_barrier_semaphore()

    def greet(dev):
        pl.semaphore_signal(barrier, inc=1, device_id=dev, device_id_type=MESH)

    for d in far_z:
        greet(ring(rem(v + d, 16)))
    for d in far_y:
        greet(at_y(rem(y + d, NY)))
    for d in far_x:
        greet(at_x(rem(x + d, NX)))
    loads = [
        pltpu.make_async_copy(a, b, lsem.at[i])
        for i, (a, b) in enumerate(((qb_h, qb), (qa_h, qa), (cache, cv), (moves_h, moves), (lens_h, lens)))
    ]
    for copy in loads:
        copy.start()
    for copy in loads:
        copy.wait()
    table = read_table(moves)
    out_to = [look(table, lambda m, r=r: (m[0] == g) & (m[1] == r)) for r in range(req)]
    came = [look(table, lambda m, k=k: (m[2] == g) & (m[3] == k)) for k in range(req)]
    length = [lens[g * req + r] for r in range(req)]

    a, _, found = came[1]
    for h in range(NG):
        last = found & (div(a, req) == h)
        qx[h] = jnp.where(last, qa[req + 1].astype(F32), qa[req].astype(F32)).astype(BF16)
    rq[v] = qx[0]
    pl.semaphore_wait(barrier, 15 + NY - 1 + NX - 1)

    def z1(d):
        to = ring(rem(v + d, 16))
        return remote(qx.at[to["group"]], rq.at[v], zs.at[2], zr.at[2], to)

    zq = remote(qb, pb, zs.at[0], zr.at[0], ring(vp))
    zp = remote(qa.at[pl.ds(0, req)], pa, zs.at[1], zr.at[1], ring(vp))
    zq.start()
    for d in far_z:
        z1(d).start()
    zp.start()

    def p1(d, c):
        h = rem(g + d, NG)
        return remote(piece(cv, h, c), st[c].at[g], p1s.at[c], p1r.at[c], at_group(h))

    for c in range(n_cuts):
        loop(1, NG, lambda d: p1(d, c).start())
    keep = [pltpu.make_async_copy(piece(cv, g, c), st[c].at[g], lsem.at[7 + c]) for c in range(n_cuts)]
    for copy in keep:
        copy.start()

    rings = ((1, 7), (2, 6), (3, 5, 4))

    def ga(u, d):
        band = min(d, NY - d, 3) - 1
        return remote(gq.at[u, x, y], gq.at[u, x, y], as_.at[u], ar.at[u, band], at_y(rem(y + d, NY)))

    def spread(u):
        for d in far_y:
            ga(u, d).start()
        relay(u, (0,))

    def relay(u, steps):
        for e in steps:
            block = gq.at[u, x, rem(y + e, NY)]
            for d in far_x:
                remote(block, block, xs.at[u], xr.at[u, d], at_x(rem(x + d, NX))).start()

    def pass_on(u, band):
        arrived(gq.at[u, x, pl.ds(0, len(rings[band]))], ar.at[u, band])
        relay(u, rings[band])

    zq.wait()
    for r in range(req):
        for i in range(2):
            mine = zl == i
            bs[0, 4 * i + 2 * r : 4 * i + 2 * r + 2] = jnp.where(mine, qb[r].astype(F32), pb[r].astype(F32))
    gq[0, x, y] = bs[0].astype(BF16)
    spread(0)
    pass_on(0, 0)
    pass_on(0, 1)

    zp.wait()
    arrived(rq.at[pl.ds(0, 15)], zr.at[2])
    for r in range(req):
        _, target, leaves = out_to[r]
        tg = div(target, req)
        for i in range(2):
            stay = jnp.where(zl == i, qa[r].astype(F32), pa[r].astype(F32))
            away = rq[(div(tg, 2) * 2 + i) * 2 + rem(tg, 2)].astype(F32)
            bs[1, 4 * i + 2 * r : 4 * i + 2 * r + 2] = jnp.where(leaves, away, stay)
    gq[1, x, y] = bs[1].astype(BF16)
    spread(1)

    n = NY * 8
    row = lax.broadcasted_iota(jnp.int32, (n, 1), 0)
    second = rem(div(row, 2), 2) == 1
    position = s * shard + lax.broadcasted_iota(jnp.int32, (n, shard), 1)

    def attend(u, i):
        q = gq[u, i].astype(F32).reshape(n, width).astype(BF16)
        scores = jnp.where(
            second,
            jnp.dot(q, cv[1], preferred_element_type=F32),
            jnp.dot(q, cv[0], preferred_element_type=F32),
        ) * SCALE
        live = position < jnp.where(second, length[1], length[0])
        masked = jnp.where(live, scores, LOW)
        top = jnp.max(masked, axis=1, keepdims=True)
        weights = jnp.where(live, jnp.exp(masked - top), 0.0)
        total = jnp.sum(weights, axis=1, keepdims=True)
        some = total > 0.0
        safe = jnp.where(some, total, 1.0)
        weights = weights * (1.0 / safe)
        part = None
        for r in range(req):
            mine = jnp.where(second == (r == 1), weights, 0.0).astype(BF16)
            term = lax.dot_general(
                mine, cv[r, :LAT, :], (((1,), (1,)), ((), ())), preferred_element_type=F32
            )
            part = term if part is None else part + term
        return part.astype(BF16), to_row(jnp.where(some, top + jnp.log(safe), LOW))

    def rc(u, d):
        to = rem(x + d, NX)
        return (remote(s1.at[u, to], r1.at[u, x], ms.at[u, 0], mr.at[u, 0], at_x(to)),
                remote(t1.at[u, to], u1.at[u, x], ms.at[u, 1], mr.at[u, 1], at_x(to)))

    def each(copies, what):
        for c in copies:
            getattr(c, what)()

    def own_block(u):
        r1[u, x], u1[u, x] = attend(u, x)

    def other_block(u, d):
        frm = rem(x + NX - d, NX)
        arrived(gq.at[u, frm], xr.at[u, d])
        s1[u, frm], t1[u, frm] = attend(u, frm)
        each(rc(u, NX - d), "start")

    def forward(c):
        keep[c].wait()
        arrived(st[c].at[pl.ds(0, NG - 1)], p1r.at[c])

        def pick(i, carry):
            d, k = div(i, req), rem(i, req)
            a, _, found = look(table, lambda m: (m[2] == d) & (m[3] == k))
            value = st[c][div(a, req), rem(a, req)]
            sel[c][d, k] = jnp.where(found, value, jnp.zeros_like(value))
            return carry

        lax.fori_loop(0, NG * req, pick, 0)
        loop(1, NG, lambda d: p2(d, c).start())
        own[c].start()

    def p2(d, c):
        h = rem(g + d, NG)
        return remote(sel[c].at[h], piece(moved, g, c), p2s.at[c], p2r.at[c], at_group(h))

    own = [pltpu.make_async_copy(sel[c].at[g], piece(moved, g, c), lsem.at[7 + n_cuts + c]) for c in range(n_cuts)]

    def re(u, d):
        to = rem(y + d, NY)
        return remote(s2.at[u, to], r2.at[u, y], ns.at[u], nr.at[u], at_y(to))

    def second_step(u):
        arrived(r1.at[u, pl.ds(0, NX - 1)], mr.at[u, 0])
        arrived(u1.at[u, pl.ds(0, NX - 1)], mr.at[u, 1])
        weights, lse = weigh([u1[u, i] for i in range(NX)])
        part = blend([r1[u, i] for i in range(NX)], [to_column(w, n) for w in weights])
        s2[u, :, :, :LAT] = part.reshape(NY, 8, LAT).astype(BF16)
        s2[u, :, :, LAT:] = tail(to_column(lse, n)).astype(F32).reshape(NY, 8, 128).astype(BF16)
        r2[u, y] = s2[u, y]
        for d in far_y:
            re(u, d).start()

    def third_step(u):
        arrived(r2.at[u, pl.ds(0, NY - 1)], nr.at[u])
        part, lse = join([r2[u, i] for i in range(NY)])
        end = tail(lse)
        for i in range(2):
            for r in range(req):
                rows = slice(4 * i + 2 * r, 4 * i + 2 * r + 2)
                s3[u, i, r, :, :LAT] = part[rows].astype(BF16)
                s3[u, i, r, :, LAT:] = end[rows]

    pass_on(0, 2)
    own_block(0)
    for band in range(3):
        pass_on(1, band)
    own_block(1)
    forward(0)
    for d in near_x:
        other_block(0, d)
    forward(1)
    for d in near_x:
        other_block(1, d)
    second_step(0)
    forward(2)
    second_step(1)

    def rf(d):
        w = rem(v + d, 16)
        to = ring(w)
        return remote(s4.at[rem(div(w, 2), 2), to["group"]], r3.at[v], os_.at[2], or_.at[2], to)

    fb = remote(s3.at[0, 1 - zl], b3.at[0], os_.at[0], or_.at[0], ring(vp))
    fa = remote(s3.at[1, 1 - zl], b3.at[1], os_.at[1], or_.at[1], ring(vp))
    stays = [pltpu.make_async_copy(s3.at[u, zl], kept.at[u], lsem.at[5]) for u in range(2)]
    fill = pltpu.make_async_copy(s3.at[1, zl, 0], r3.at[v], lsem.at[6])
    third_step(1)
    _, target, leaves = out_to[1]
    for i in range(2):
        for h in range(NG):
            last = leaves & (div(target, req) == h)
            s4[i, h] = jnp.where(last, s3[1, i, 1], s3[1, i, 0])
    for d in far_z:
        rf(d).start()
    fa.start()
    fill.start()
    third_step(0)
    fb.start()
    for copy in stays:
        copy.start()
    fb.wait()
    fa.wait()
    fill.wait()
    pltpu.make_async_copy(kept, kept, lsem.at[5]).wait()
    arrived(r3.at[pl.ds(0, 15)], or_.at[2])
    for c in range(n_cuts):
        own[c].wait()
        arrived(sel[c].at[pl.ds(0, NG - 1)], p2r.at[c])

    left(rq.at[pl.ds(0, 15)], zs.at[2])
    left(r3.at[pl.ds(0, 15)], os_.at[2])
    for u in range(2):
        left(gq.at[u, x, pl.ds(0, NY - 1)], as_.at[u])
        left(gq.at[u, pl.ds(0, NX - 1)], xs.at[u])
        left(s1.at[u, pl.ds(0, NX - 1)], ms.at[u, 0])
        left(t1.at[u, pl.ds(0, NX - 1)], ms.at[u, 1])
        left(s2.at[u, pl.ds(0, NY - 1)], ns.at[u])
    for c in range(n_cuts):
        left(st[c].at[pl.ds(0, NG - 1)], p1s.at[c])
        left(sel[c].at[pl.ds(0, NG - 1)], p2s.at[c])


def finish(lens_h, moves_h, mine_h, b3_h, r3_h, moved, ob_h, lb_h, oa_h, la_h, moved_to,
           lens, moves, mine, b3, r3, ob, lb, oa, la, hold, sems):
    req = ob.shape[0]
    g, zl = lax.axis_index("group"), rem(lax.axis_index("seq"), 2)
    takes = [pltpu.make_async_copy(moved.at[r], hold.at[r], sems.at[0, r]) for r in range(req)]
    puts = [pltpu.make_async_copy(hold.at[r], moved_to.at[r], sems.at[1, r]) for r in range(req)]
    loads = [
        pltpu.make_async_copy(a, b, sems.at[0, req + i])
        for i, (a, b) in enumerate(((lens_h, lens), (moves_h, moves), (mine_h, mine), (b3_h, b3), (r3_h, r3)))
    ]
    stores = [
        pltpu.make_async_copy(a, b, sems.at[1, req + i])
        for i, (a, b) in enumerate(((ob, ob_h), (lb, lb_h), (oa, oa_h), (la, la_h)))
    ]
    for copy in takes + loads:
        copy.start()
    for copy in loads:
        copy.wait()
    table = read_table(moves)
    for r in range(req):
        alive = lens[g * req + r] > 0
        out, lse = join([mine[0, r], b3[0, r]])
        ob[r] = jnp.where(alive, out, 0.0).astype(BF16)
        lb[r : r + 1, :] = to_row(jnp.where(alive, lse, 0.0))[:, 0:2]
        _, _, leaves = look(table, lambda m, r=r: (m[0] == g) & (m[1] == r))
        stays = alive & jnp.logical_not(leaves)
        out, lse = join([mine[1, r], b3[1, r]])
        oa[r] = jnp.where(stays, out, 0.0).astype(BF16)
        la[:, r : r + 1] = jnp.where(stays, lse, 0.0)
    for copy, put in zip(takes, puts):
        copy.wait()
        put.start()
    for k in range(req):
        a, _, found = look(table, lambda m, k=k: (m[2] == g) & (m[3] == k))
        sg = div(a, req)
        out, lse = join([r3[(div(sg, 2) * 2 + i) * 2 + rem(sg, 2)] for i in range(2)])
        alive = found & (lens[a] > 0)
        oa[req + k] = jnp.where(alive, out, 0.0).astype(BF16)
        la[:, req + k : req + k + 1] = jnp.where(alive, lse, 0.0)
    for copy in stores:
        copy.start()
    for copy in stores + puts:
        copy.wait()


def local(cache, lengths, moves, qb, qa):
    req, shard, width = cache.shape
    heads = qb.shape[1]
    n = NY * 8
    wide = LAT + 128
    vm, dma = pltpu.VMEM, pltpu.SemaphoreType.DMA
    hbm = pl.BlockSpec(memory_space=pltpu.HBM)
    shape = jax.ShapeDtypeStruct
    outs = (
        shape((req, heads, LAT), BF16),
        shape((req, heads), F32),
        shape((2 * req, heads, LAT), BF16),
        shape((heads, 2 * req), F32),
        shape((req, width, shard), BF16),
    )
    sent = (
        shape((2, req, heads, wide), BF16),
        shape((2, req, heads, wide), BF16),
        shape((16, heads, wide), BF16),
        outs[4],
    )
    moves = moves.T
    got = pl.pallas_call(
        kernel,
        out_shape=sent,
        in_specs=[hbm] * 5,
        out_specs=(hbm,) * 4,
        scratch_shapes=[
            pltpu.SMEM(lengths.shape, jnp.int32),
            pltpu.SMEM(moves.shape, jnp.int32),
            vm(qb.shape, BF16),
            vm(qa.shape, BF16),
            vm((req, width, shard), BF16),
            *[tuple(vm((NG, req, size, 128), BF16) for size in CUTS)] * 2,
            vm((16, heads, width), BF16),
            vm((NG, heads, width), BF16),
            vm((req, heads, width), BF16),
            vm((req, heads, width), BF16),
            vm((2, 8, width), F32),
            vm((2, NX, NY, 8, width), BF16),
            vm((2, NX, n, LAT), BF16), vm((2, NX, n, LAT), BF16),
            vm((2, NX, 1, 128), F32), vm((2, NX, 1, 128), F32),
            vm((2, NY, 8, wide), BF16), vm((2, NY, 8, wide), BF16),
            vm((2, 2, req, heads, wide), BF16),
            vm((2, NG, heads, wide), BF16),
            dma((7 + 2 * len(CUTS),)),
            *[dma((len(CUTS),))] * 4,
            dma((3,)), dma((3,)),
            dma((2,)), dma((2, 3)),
            dma((2,)), dma((2, NX)),
            dma((2, 2)), dma((2, 2)),
            dma((2,)), dma((2,)),
            dma((3,)), dma((3,)),
        ],
        name="decode_and_move",
        compiler_params=pltpu.CompilerParams(
            collective_id=0, has_side_effects=True, vmem_limit_bytes=63 << 20
        ),
    )(lengths, moves, jnp.transpose(cache, (0, 2, 1)), qb, qa)
    ob, lb, oa, la, moved = pl.pallas_call(
        finish,
        out_shape=outs,
        in_specs=[hbm] * 6,
        out_specs=(hbm,) * 5,
        scratch_shapes=[
            pltpu.SMEM(lengths.shape, jnp.int32),
            pltpu.SMEM(moves.shape, jnp.int32),
            *(vm(o.shape, o.dtype) for o in sent[:3]),
            *(vm(o.shape, o.dtype) for o in outs),
            dma((2, req + 5)),
        ],
        name="finish",
        compiler_params=pltpu.CompilerParams(vmem_limit_bytes=63 << 20),
    )(lengths, moves, *got)
    return ob, lb, oa, la.T, jnp.transpose(moved, (0, 2, 1))


def solution(mesh):
    placed = (P("group", "seq", None), P(), P(), P("group", "seq", None), P("group", "seq", None))
    return jax.shard_map(
        local,
        mesh=mesh,
        in_specs=placed,
        out_specs=(
            P("group", "seq", None),
            P("group", "seq"),
            P("group", "seq", None),
            P("group", "seq"),
            P("group", "seq", None),
        ),
        check_vma=False,
    )
```

time: 56.4 us -> 51.3 us (0.910)
  Pallas kernels: 55.6 us -> 50.5 us
    pallas_call x2, Pallas kernels: 55.6 us -> 50.5 us  [the longest x1 48.4 us: local(): pl.pallas_call(kernel, out_shape=sent, in_specs=[hbm] * 5, out_specs=(hbm...]
where the time goes in v3:
time: 51.3 us; the launch traced here: 51.1 us
  Pallas kernels  50.5 us (98%)
  between operations  0.64 us (1%)
    pallas_call x1, Pallas kernels, local(): pl.pallas_call(kernel, out_shape=sent, in_specs=[hbm] * 5, out_specs=(hbm...  48.4 us
    pallas_call x1, Pallas kernels, local(): pl.pallas_call(finish, out_shape=outs, in_specs=[hbm] * 6, out_specs=(hbm...  2.05 us

profile of v3, /device:TPU:1, one launch (start us, length us, event | category | flops | bytes accessed | tf_op | source)
XLA Modules:
  0.0 51.1 jit_solution(1530214265074150846)
XLA Ops:
  0.6 48.4 %decode_and_move.1 = (bf16[2,2,2,640]{3,2,1,0:T(2,128)(2,1)}, bf16[2,2,2,640]{3,2,1,0:T(2,128)(2,1)}, bf16[16,2,640]{2,1,0:T(2,128)(2,1)}, bf16[2,576,256]{2,1,0:T(8,128)(2,1)}) custom-call(s32[16]{0:T(128)} %lens_h.3, s32[4,12]{1,0:T(4,128)} %bitcast.5, bf16[2,576,256]{2,1,0:T(8,128)(2,1)} %bitcast.4, bf16[2,2,576]{2,1,0:T(2,128)(2,1)} %qb_h.1, ...), custom_call_target="tpu_custom_call" | custom-call | tf_op jit(solution)/shard_map/decode_and_move/pallas_call | solution.py:462
  49.1 2.0 %finish.1 = (bf16[2,2,512]{2,1,0:T(2,128)(2,1)}, f32[2,2]{1,0:T(2,128)}, bf16[4,2,512]{2,1,0:T(2,128)(2,1)}, f32[2,4]{1,0:T(2,128)}, bf16[2,576,256]{2,1,0:T(8,128)(2,1)}) custom-call(s32[16]{0:T(128)} %lens_h.3, s32[4,12]{1,0:T(4,128)} %bitcast.6, bf16[2,2,2,640]{3,2,1,0:T(2,128)(2,1)} %get-tuple-element.14.mine_h, ...), custom_call_target="tpu_custom_call" | custom-call | tf_op jit(solution)/shard_map/finish/pallas_call | solution.py:499

commit v4 on v3

--- a/solution.py
+++ b/solution.py
@@ -191,38 +191,41 @@
         return remote(piece(cv, h, c), st[c].at[g], p1s.at[c], p1r.at[c], at_group(h))
 
     for c in range(n_cuts):
-        loop(1, NG, lambda d: p1(d, c).start())
+        loop(0, 7, lambda k: p1((4, 5, 3, 2, 6, 7, 1)[k], c).start())
     keep = [pltpu.make_async_copy(piece(cv, g, c), st[c].at[g], lsem.at[7 + c]) for c in range(n_cuts)]
     for copy in keep:
         copy.start()
 
-    rings = ((1, 7), (2, 6), (3, 5, 4))
+    steps = (0, 1, 7, 2, 6, 3, 4, 5)
+    bands = (pl.ds(0, 1), pl.ds(1, 2), pl.ds(3, 2), pl.ds(5, 3))
+
+    def slot(d):
+        return steps.index(d % NY)
 
     def ga(u, d):
         band = min(d, NY - d, 3) - 1
-        return remote(gq.at[u, x, y], gq.at[u, x, y], as_.at[u], ar.at[u, band], at_y(rem(y + d, NY)))
+        return remote(gq.at[u, x, 0], gq.at[u, x, slot(-d)], as_.at[u], ar.at[u, band], at_y(rem(y + d, NY)))
 
     def spread(u):
         for d in far_y:
             ga(u, d).start()
-        relay(u, (0,))
-
-    def relay(u, steps):
-        for e in steps:
-            block = gq.at[u, x, rem(y + e, NY)]
-            for d in far_x:
-                remote(block, block, xs.at[u], xr.at[u, d], at_x(rem(x + d, NX))).start()
+        relay(u, 0)
+
+    def relay(u, band):
+        part = gq.at[u, x, bands[band]]
+        for d in far_x:
+            remote(part, part, xs.at[u], xr.at[u, d], at_x(rem(x + d, NX))).start()
 
     def pass_on(u, band):
-        arrived(gq.at[u, x, pl.ds(0, len(rings[band]))], ar.at[u, band])
-        relay(u, rings[band])
+        arrived(gq.at[u, x, bands[band + 1]], ar.at[u, band])
+        relay(u, band + 1)
 
     zq.wait()
     for r in range(req):
         for i in range(2):
             mine = zl == i
             bs[0, 4 * i + 2 * r : 4 * i + 2 * r + 2] = jnp.where(mine, qb[r].astype(F32), pb[r].astype(F32))
-    gq[0, x, y] = bs[0].astype(BF16)
+    gq[0, x, 0] = bs[0].astype(BF16)
     spread(0)
     pass_on(0, 0)
     pass_on(0, 1)
@@ -236,16 +239,18 @@
             stay = jnp.where(zl == i, qa[r].astype(F32), pa[r].astype(F32))
             away = rq[(div(tg, 2) * 2 + i) * 2 + rem(tg, 2)].astype(F32)
             bs[1, 4 * i + 2 * r : 4 * i + 2 * r + 2] = jnp.where(leaves, away, stay)
-    gq[1, x, y] = bs[1].astype(BF16)
+    gq[1, x, 0] = bs[1].astype(BF16)
     spread(1)
 
     n = NY * 8
-    row = lax.broadcasted_iota(jnp.int32, (n, 1), 0)
-    second = rem(div(row, 2), 2) == 1
-    position = s * shard + lax.broadcasted_iota(jnp.int32, (n, shard), 1)
-
-    def attend(u, i):
-        q = gq[u, i].astype(F32).reshape(n, width).astype(BF16)
+
+    def attend(u, sources):
+        m = n * len(sources)
+        row = lax.broadcasted_iota(jnp.int32, (m, 1), 0)
+        second = rem(div(row, 2), 2) == 1
+        position = s * shard + lax.broadcasted_iota(jnp.int32, (m, shard), 1)
+        blocks = [gq[u, i].astype(F32).reshape(n, width) for i in sources]
+        q = (blocks[0] if len(blocks) == 1 else jnp.concatenate(blocks, axis=0)).astype(BF16)
         scores = jnp.where(
             second,
             jnp.dot(q, cv[1], preferred_element_type=F32),
@@ -266,10 +271,10 @@
                 mine, cv[r, :LAT, :], (((1,), (1,)), ((), ())), preferred_element_type=F32
             )
             part = term if part is None else part + term
-        return part.astype(BF16), to_row(jnp.where(some, top + jnp.log(safe), LOW))
-
-    def rc(u, d):
-        to = rem(x + d, NX)
+        part, lse = part.astype(BF16), jnp.where(some, top + jnp.log(safe), LOW)
+        return [(part[n * k : n * k + n], to_row(lse[n * k : n * k + n])) for k in range(len(sources))]
+
+    def rc(u, to):
         return (remote(s1.at[u, to], r1.at[u, x], ms.at[u, 0], mr.at[u, 0], at_x(to)),
                 remote(t1.at[u, to], u1.at[u, x], ms.at[u, 1], mr.at[u, 1], at_x(to)))
 
@@ -277,14 +282,22 @@
         for c in copies:
             getattr(c, what)()
 
-    def own_block(u):
-        r1[u, x], u1[u, x] = attend(u, x)
-
-    def other_block(u, d):
-        frm = rem(x + NX - d, NX)
-        arrived(gq.at[u, frm], xr.at[u, d])
-        s1[u, frm], t1[u, frm] = attend(u, frm)
-        each(rc(u, NX - d), "start")
+    def blocks(u, steps):
+        sources = [rem(x + NX - d, NX) for d in steps]
+        for d, frm in zip(steps, sources):
+            if d:
+                arrived(gq.at[u, frm], xr.at[u, d])
+        for d, frm, (part, lse) in zip(steps, sources, attend(u, sources)):
+            if d:
+                s1[u, frm], t1[u, frm] = part, lse
+                each(rc(u, frm), "start")
+            else:
+                r1[u, x], u1[u, x] = part, lse
+
+    def block_from(u, frm):
+        arrived(gq.at[u, frm], xr.at[u, rem(x + NX - frm, NX)])
+        [(s1[u, frm], t1[u, frm])] = attend(u, [frm])
+        each(rc(u, frm), "start")
 
     def forward(c):
         keep[c].wait()
@@ -298,7 +311,7 @@
             return carry
 
         lax.fori_loop(0, NG * req, pick, 0)
-        loop(1, NG, lambda d: p2(d, c).start())
+        loop(0, 7, lambda k: p2((4, 5, 3, 2, 6, 7, 1)[k], c).start())
         own[c].start()
 
     def p2(d, c):
@@ -308,8 +321,7 @@
     own = [pltpu.make_async_copy(sel[c].at[g], piece(moved, g, c), lsem.at[7 + n_cuts + c]) for c in range(n_cuts)]
 
     def re(u, d):
-        to = rem(y + d, NY)
-        return remote(s2.at[u, to], r2.at[u, y], ns.at[u], nr.at[u], at_y(to))
+        return remote(s2.at[u, slot(d)], r2.at[u, slot(-d)], ns.at[u], nr.at[u], at_y(rem(y + d, NY)))
 
     def second_step(u):
         arrived(r1.at[u, pl.ds(0, NX - 1)], mr.at[u, 0])
@@ -318,7 +330,7 @@
         part = blend([r1[u, i] for i in range(NX)], [to_column(w, n) for w in weights])
         s2[u, :, :, :LAT] = part.reshape(NY, 8, LAT).astype(BF16)
         s2[u, :, :, LAT:] = tail(to_column(lse, n)).astype(F32).reshape(NY, 8, 128).astype(BF16)
-        r2[u, y] = s2[u, y]
+        r2[u, 0] = s2[u, 0]
         for d in far_y:
             re(u, d).start()
 
@@ -333,16 +345,14 @@
                 s3[u, i, r, :, LAT:] = end[rows]
 
     pass_on(0, 2)
-    own_block(0)
     for band in range(3):
         pass_on(1, band)
-    own_block(1)
+    blocks(1, (0,))
     forward(0)
-    for d in near_x:
-        other_block(0, d)
+    blocks(0, (1, 3, 2, 0))
     forward(1)
-    for d in near_x:
-        other_block(1, d)
+    for j in range(NX - 1):
+        block_from(1, jnp.where(x <= j, j + 1, j))
     second_step(0)
     forward(2)
     second_step(1)

time: 51.3 us -> 50.5 us (0.984)
  Pallas kernels: 50.5 us -> 49.7 us
    pallas_call x1, Pallas kernels: 48.4 us -> 47.6 us  [local(): pl.pallas_call(kernel, out_shape=sent, in_specs=[hbm] * 5, out_specs=(hbm...]
where the time goes in v4:
time: 50.5 us; the launch traced here: 50.3 us
  Pallas kernels  49.7 us (98%)
  between operations  0.64 us (1%)
    pallas_call x1, Pallas kernels, local(): pl.pallas_call(kernel, out_shape=sent, in_specs=[hbm] * 5, out_specs=(hbm...  47.6 us
    pallas_call x1, Pallas kernels, local(): pl.pallas_call(finish, out_shape=outs, in_specs=[hbm] * 6, out_specs=(hbm...  2.05 us

profile of v4, /device:TPU:1, one launch (start us, length us, event | category | flops | bytes accessed | tf_op | source)
XLA Modules:
  0.0 50.3 jit_solution(16355088494300713338)
XLA Ops:
  0.6 47.6 %decode_and_move.1 = (bf16[2,2,2,640]{3,2,1,0:T(2,128)(2,1)}, bf16[2,2,2,640]{3,2,1,0:T(2,128)(2,1)}, bf16[16,2,640]{2,1,0:T(2,128)(2,1)}, bf16[2,576,256]{2,1,0:T(8,128)(2,1)}) custom-call(s32[16]{0:T(128)} %lens_h.3, s32[4,12]{1,0:T(4,128)} %bitcast.5, bf16[2,576,256]{2,1,0:T(8,128)(2,1)} %bitcast.4, bf16[2,2,576]{2,1,0:T(2,128)(2,1)} %qb_h.1, ...), custom_call_target="tpu_custom_call" | custom-call | tf_op jit(solution)/shard_map/decode_and_move/pallas_call | solution.py:472
  48.2 2.0 %finish.1 = (bf16[2,2,512]{2,1,0:T(2,128)(2,1)}, f32[2,2]{1,0:T(2,128)}, bf16[4,2,512]{2,1,0:T(2,128)(2,1)}, f32[2,4]{1,0:T(2,128)}, bf16[2,576,256]{2,1,0:T(8,128)(2,1)}) custom-call(s32[16]{0:T(128)} %lens_h.3, s32[4,12]{1,0:T(4,128)} %bitcast.6, bf16[2,2,2,640]{3,2,1,0:T(2,128)(2,1)} %get-tuple-element.14.mine_h, ...), custom_call_target="tpu_custom_call" | custom-call | tf_op jit(solution)/shard_map/finish/pallas_call | solution.py:509

commit v5 on v4

--- a/solution.py
+++ b/solution.py
@@ -96,7 +96,7 @@
 
 
 def kernel(lens_h, moves_h, cache, qb_h, qa_h, kept, b3, r3, moved,
-           lens, moves, qb, qa, cv, st, sel, rq, qx, pb, pa, bs, gq,
+           lens, moves, plan, qb, qa, cv, st, sel, rq, qx, pb, pa, bs, gq,
            s1, r1, t1, u1, s2, r2, s3, s4,
            lsem, p1s, p1r, p2s, p2r, zs, zr, as_, ar, xs, xr, ms, mr, ns, nr, os_, or_):
     req, width, shard = cv.shape
@@ -167,6 +167,13 @@
     out_to = [look(table, lambda m, r=r: (m[0] == g) & (m[1] == r)) for r in range(req)]
     came = [look(table, lambda m, k=k: (m[2] == g) & (m[3] == k)) for k in range(req)]
     length = [lens[g * req + r] for r in range(req)]
+
+    def note(i, carry):
+        a, _, found = look(table, lambda m: m[2] * req + m[3] == i)
+        plan[0, i], plan[1, i], plan[2, i] = div(a, req), rem(a, req), found.astype(jnp.int32)
+        return carry
+
+    lax.fori_loop(0, NG * req, note, 0)
 
     a, _, found = came[1]
     for h in range(NG):
@@ -304,10 +311,8 @@
         arrived(st[c].at[pl.ds(0, NG - 1)], p1r.at[c])
 
         def pick(i, carry):
-            d, k = div(i, req), rem(i, req)
-            a, _, found = look(table, lambda m: (m[2] == d) & (m[3] == k))
-            value = st[c][div(a, req), rem(a, req)]
-            sel[c][d, k] = jnp.where(found, value, jnp.zeros_like(value))
+            value = st[c][plan[0, i], plan[1, i]]
+            sel[c][div(i, req), rem(i, req)] = jnp.where(plan[2, i] > 0, value, jnp.zeros_like(value))
             return carry
 
         lax.fori_loop(0, NG * req, pick, 0)
@@ -350,9 +355,9 @@
     blocks(1, (0,))
     forward(0)
     blocks(0, (1, 3, 2, 0))
-    forward(1)
     for j in range(NX - 1):
         block_from(1, jnp.where(x <= j, j + 1, j))
+    forward(1)
     second_step(0)
     forward(2)
     second_step(1)
@@ -477,6 +482,7 @@
         scratch_shapes=[
             pltpu.SMEM(lengths.shape, jnp.int32),
             pltpu.SMEM(moves.shape, jnp.int32),
+            pltpu.SMEM((3, NG * req), jnp.int32),
             vm(qb.shape, BF16),
             vm(qa.shape, BF16),
             vm((req, width, shard), BF16),

time: 50.5 us -> 50 us (0.990)
  no operation moved by 1% of the time
where the time goes in v5:
time: 50 us; the launch traced here: 49.9 us
  Pallas kernels  49.2 us (98%)
  between operations  0.64 us (1%)
    pallas_call x1, Pallas kernels, local(): pl.pallas_call(kernel, out_shape=sent, in_specs=[hbm] * 5, out_specs=(hbm...  47.2 us
    pallas_call x1, Pallas kernels, local(): pl.pallas_call(finish, out_shape=outs, in_specs=[hbm] * 6, out_specs=(hbm...  2.05 us

profile of v5, /device:TPU:1, one launch (start us, length us, event | category | flops | bytes accessed | tf_op | source)
XLA Modules:
  0.0 49.9 jit_solution(9717622119900481763)
XLA Ops:
  0.6 47.2 %decode_and_move.1 = (bf16[2,2,2,640]{3,2,1,0:T(2,128)(2,1)}, bf16[2,2,2,640]{3,2,1,0:T(2,128)(2,1)}, bf16[16,2,640]{2,1,0:T(2,128)(2,1)}, bf16[2,576,256]{2,1,0:T(8,128)(2,1)}) custom-call(s32[16]{0:T(128)} %lens_h.3, s32[4,12]{1,0:T(4,128)} %bitcast.5, bf16[2,576,256]{2,1,0:T(8,128)(2,1)} %bitcast.4, bf16[2,2,576]{2,1,0:T(2,128)(2,1)} %qb_h.1, ...), custom_call_target="tpu_custom_call" | custom-call | tf_op jit(solution)/shard_map/decode_and_move/pallas_call | solution.py:477
  47.8 2.0 %finish.1 = (bf16[2,2,512]{2,1,0:T(2,128)(2,1)}, f32[2,2]{1,0:T(2,128)}, bf16[4,2,512]{2,1,0:T(2,128)(2,1)}, f32[2,4]{1,0:T(2,128)}, bf16[2,576,256]{2,1,0:T(8,128)(2,1)}) custom-call(s32[16]{0:T(128)} %lens_h.3, s32[4,12]{1,0:T(4,128)} %bitcast.6, bf16[2,2,2,640]{3,2,1,0:T(2,128)(2,1)} %get-tuple-element.14.mine_h, ...), custom_call_target="tpu_custom_call" | custom-call | tf_op jit(solution)/shard_map/finish/pallas_call | solution.py:515

commit v6 on v5

--- a/solution.py
+++ b/solution.py
@@ -149,10 +149,12 @@
     def greet(dev):
         pl.semaphore_signal(barrier, inc=1, device_id=dev, device_id_type=MESH)
 
-    for d in far_z:
+    for d in far_z[:6]:
         greet(ring(rem(v + d, 16)))
     for d in far_y:
         greet(at_y(rem(y + d, NY)))
+    for d in far_z[6:]:
+        greet(ring(rem(v + d, 16)))
     for d in far_x:
         greet(at_x(rem(x + d, NX)))
     loads = [
@@ -359,8 +361,8 @@
         block_from(1, jnp.where(x <= j, j + 1, j))
     forward(1)
     second_step(0)
+    second_step(1)
     forward(2)
-    second_step(1)
 
     def rf(d):
         w = rem(v + d, 16)

time: 50 us -> 50.1 us (level)
  no operation moved by 1% of the time
where the time goes in v6:
time: 50.1 us; the launch traced here: 49.9 us
  Pallas kernels  49.3 us (98%)
  between operations  0.64 us (1%)
    pallas_call x1, Pallas kernels, local(): pl.pallas_call(kernel, out_shape=sent, in_specs=[hbm] * 5, out_specs=(hbm...  47.2 us
    pallas_call x1, Pallas kernels, local(): pl.pallas_call(finish, out_shape=outs, in_specs=[hbm] * 6, out_specs=(hbm...  2.05 us

profile of v6, /device:TPU:1, one launch (start us, length us, event | category | flops | bytes accessed | tf_op | source)
XLA Modules:
  0.0 49.9 jit_solution(18154416168543205578)
XLA Ops:
  0.6 47.2 %decode_and_move.1 = (bf16[2,2,2,640]{3,2,1,0:T(2,128)(2,1)}, bf16[2,2,2,640]{3,2,1,0:T(2,128)(2,1)}, bf16[16,2,640]{2,1,0:T(2,128)(2,1)}, bf16[2,576,256]{2,1,0:T(8,128)(2,1)}) custom-call(s32[16]{0:T(128)} %lens_h.3, s32[4,12]{1,0:T(4,128)} %bitcast.5, bf16[2,576,256]{2,1,0:T(8,128)(2,1)} %bitcast.4, bf16[2,2,576]{2,1,0:T(2,128)(2,1)} %qb_h.1, ...), custom_call_target="tpu_custom_call" | custom-call | tf_op jit(solution)/shard_map/decode_and_move/pallas_call | solution.py:479
  47.9 2.0 %finish.1 = (bf16[2,2,512]{2,1,0:T(2,128)(2,1)}, f32[2,2]{1,0:T(2,128)}, bf16[4,2,512]{2,1,0:T(2,128)(2,1)}, f32[2,4]{1,0:T(2,128)}, bf16[2,576,256]{2,1,0:T(8,128)(2,1)}) custom-call(s32[16]{0:T(128)} %lens_h.3, s32[4,12]{1,0:T(4,128)} %bitcast.6, bf16[2,2,2,640]{3,2,1,0:T(2,128)(2,1)} %get-tuple-element.14.mine_h, ...), custom_call_target="tpu_custom_call" | custom-call | tf_op jit(solution)/shard_map/finish/pallas_call | solution.py:517
